TPU v7x, 32 devices: a whole 2x2x4 slice. The times are simulated.
32 devices in a mesh: dp: 8 (over y, x, core), mp: 4 (over z).
Axes of the slice: x: 2, y: 2, z: 4, core: 2. Of those that a mesh axis runs over, the one named last changes fastest.
Arguments:
- inputs: bfloat16 [512, 65536], P('mp', 'dp'), may hold values from -24 to 24
- cotangent: bfloat16 [512, 65536], P('mp', 'dp'), may hold values from -4 to 4
- member_mask: int32 [2048, 32], P('dp'), may hold values from 0 to 1, as said below
- members: float32 [6, 32, 512], P(None, 'dp', 'mp'), may hold values from -3 to 3
- first_moment: float32 [6, 32, 512], P(None, 'dp', 'mp')
- second_moment: float32 [6, 32, 512], P(None, 'dp', 'mp'), as said below
- first_weight: float32 [512, 512], P('dp', 'mp'), may hold values from -0.25 to 0.25
- second_weight: float32 [512, 512], P('mp', 'dp'), may hold values from -0.25 to 0.25
- first_left: float32 [512, 512], P('dp', 'mp')
- first_right: float32 [512, 512], P('dp', 'mp')
- second_left: float32 [512, 512], P('mp', 'dp')
- second_right: float32 [512, 512], P('mp', 'dp')
- first_left_root: float32 [512, 512], P('dp')
- first_right_root: float32 [512, 512], P('mp')
- second_left_root: float32 [512, 512], P('mp')
- second_right_root: float32 [512, 512], P('dp')
Outputs:
- logits: bfloat16 [512, 65536], P('mp', 'dp')
- input_grad: bfloat16 [512, 65536], P('mp', 'dp')
- rms_stats: float32 [2], replicated
- first_grad: float32 [512, 512], P('dp', 'mp')
- first_new: float32 [512, 512], P('dp', 'mp')
- first_left_new: float32 [512, 512], P('dp', 'mp')
- first_right_new: float32 [512, 512], P('dp', 'mp')
- second_grad: float32 [512, 512], P('mp', 'dp')
- second_new: float32 [512, 512], P('mp', 'dp')
- second_left_new: float32 [512, 512], P('mp', 'dp')
- second_right_new: float32 [512, 512], P('mp', 'dp')
- moment_one_new: float32 [6, 32, 512], P(None, 'dp', 'mp')
- moment_two_new: float32 [6, 32, 512], P(None, 'dp', 'mp')
- members_new: float32 [6, 32, 512], P(None, 'dp', 'mp')
Inputs may be any that keep to these rules, and one draw needn't show every extreme that they name: `member_mask`: each object has between 8 and 32 trained members; some object has exactly 8 and some exactly 32. `second_moment`: positive.
All inputs are finite; a program needn't handle non-finite values.
Results may differ from a plain program's by a relative error of at most 0.0087.
Values may be sent and summed in bfloat16 or wider, within the bound.
A program may use at most 128 MiB of HBM per device.

v0:
```python
import jax
import jax.numpy as jnp
from jax import lax
from jax.sharding import PartitionSpec as P

D = 512
K = 32
STEP = 10


beta_first = 0.9
beta_second = 0.999
adam_eps = 1e-08
adam_rate = 0.2
stat_decay = 0.95
shampoo_rate = 1.0
over_rows = (((0,), (0,)), ((), ()))
over_cols = (((1,), (1,)), ((), ()))


def group_count(values):
    objects = values.shape[1] // K
    repeat = max(1, 128 // K)
    return repeat


def tiled_table(table, repeat):
    return jnp.tile(table.T, (1, repeat))


def by_member(values, table):
    width = values.shape[0]
    repeat = group_count(values)
    shaped = values.reshape(width, -1, repeat * K)
    return (shaped * tiled_table(table, repeat)[:, None, :]).reshape(values.shape)


def member_affine(values, gain, bias):
    width = values.shape[0]
    repeat = group_count(values)
    shaped = values.reshape(width, -1, repeat * K)
    return (
        shaped * tiled_table(gain, repeat)[:, None, :] + tiled_table(bias, repeat)[:, None, :]
    ).reshape(values.shape)


def member_sum(values):
    width = values.shape[0]
    repeat = group_count(values)
    partial_value = values.reshape(width, -1, repeat * K).sum(1)
    return partial_value.reshape(width, repeat, K).sum(1).T


def middle_forward(rows_in, first_low, second_low, gain_in, bias_in, row_mid):
    hidden_pre = lax.dot_general(first_low, rows_in, over_rows, preferred_element_type=jnp.float32)
    shifted = member_affine(hidden_pre, gain_in, bias_in)
    hidden, gelu_pull = jax.vjp(jax.nn.gelu, shifted)
    hidden_in = by_member(hidden, row_mid).astype(jnp.bfloat16)
    partial_value = lax.dot_general(
        second_low, hidden_in, over_rows, preferred_element_type=jnp.float32
    )
    return (hidden_pre, hidden, gelu_pull, hidden_in, partial_value)


def middle_backward(
    grad_rows,
    rows_in,
    first_low,
    second_low,
    gain_in,
    row_mid,
    hidden_pre,
    hidden,
    gelu_pull,
    hidden_in,
):
    grad_second = lax.dot_general(
        hidden_in, grad_rows, over_cols, preferred_element_type=jnp.float32
    )
    grad_hidin = jnp.dot(second_low, grad_rows, preferred_element_type=jnp.float32)
    grad_row_mid = member_sum(grad_hidin * hidden)
    grad_shift = gelu_pull(by_member(grad_hidin, row_mid))[0]
    grad_bias_in = member_sum(grad_shift)
    grad_gain_in = member_sum(grad_shift * hidden_pre)
    grad_pre = by_member(grad_shift, gain_in).astype(jnp.bfloat16)
    grad_first = lax.dot_general(rows_in, grad_pre, over_cols, preferred_element_type=jnp.float32)
    row_back = jnp.dot(first_low, grad_pre, preferred_element_type=jnp.float32)
    return (
        grad_first,
        grad_second,
        jnp.stack([grad_gain_in, grad_bias_in, grad_row_mid]),
        row_back,
    )


def on_device(
    inputs,
    cotangent,
    member_mask,
    members,
    first_moment,
    second_moment,
    first_weight,
    second_weight,
    first_left,
    first_right,
    second_left,
    second_right,
    first_left_root,
    first_right_root,
    second_left_root,
    second_right_root,
):
    high = lax.Precision.HIGHEST
    first_block, second_block, member_cols = (
        lax.all_gather(first_weight, "dp", axis=0, tiled=True),
        lax.all_gather(second_weight, "dp", axis=1, tiled=True),
        lax.all_gather(members, "dp", axis=1, tiled=True),
    )
    row_in = member_cols[0]
    gain_out = member_cols[4]
    bias_out = member_cols[5]
    values = inputs.astype(jnp.float32)
    weight_mask = member_mask.astype(jnp.float32).reshape(1, -1)
    scaled = by_member(values, row_in).astype(jnp.bfloat16)
    first_low = first_block.astype(jnp.bfloat16)
    second_low = second_block.astype(jnp.bfloat16)
    hidden_tables = member_cols[1:4]
    gathered = lax.all_gather(scaled, "mp", axis=0, tiled=True)
    hidden_pre, hidden, gelu_pull, hidden_in, partial_value = middle_forward(
        gathered, first_low, second_low, hidden_tables[0], hidden_tables[1], hidden_tables[2]
    )
    projected = lax.psum_scatter(partial_value, "mp", scatter_dimension=0, tiled=True)
    branch = member_affine(projected, gain_out, bias_out)
    logits = (values + branch).astype(jnp.bfloat16)
    first_column = (lax.axis_index("mp") == 0).astype(jnp.float32)
    totals = lax.psum(
        (
            jnp.sum(weight_mask * values * values),
            jnp.sum(weight_mask * branch * branch),
            jnp.sum(weight_mask) * first_column,
        ),
        ("dp", "mp"),
    )
    rms_stats = jnp.sqrt(jnp.stack([totals[0], totals[1]]) / (totals[2] * D))
    grad_out = cotangent.astype(jnp.float32) * weight_mask
    grad_bias_out = member_sum(grad_out)
    grad_gain_out = member_sum(grad_out * projected)
    grad_proj = by_member(grad_out, gain_out).astype(jnp.bfloat16)
    grad_full = lax.all_gather(grad_proj, "mp", axis=0, tiled=True)
    grad_first, grad_second, mid_grads, partial_back = middle_backward(
        grad_full,
        gathered,
        first_low,
        second_low,
        hidden_tables[0],
        hidden_tables[2],
        hidden_pre,
        hidden,
        gelu_pull,
        hidden_in,
    )
    grad_scaled = lax.psum_scatter(partial_back, "mp", scatter_dimension=0, tiled=True)
    grad_row_in = member_sum(grad_scaled * values)
    input_grad = (by_member(grad_scaled, row_in) + grad_out).astype(jnp.bfloat16)
    grad_vec = jnp.concatenate(
        [grad_row_in[None], mid_grads, grad_gain_out[None], grad_bias_out[None]], axis=0
    )
    first_grad, second_grad, vec_grad = (
        lax.psum_scatter(grad_first, "dp", scatter_dimension=0, tiled=True),
        lax.psum_scatter(grad_second, "dp", scatter_dimension=1, tiled=True),
        lax.psum_scatter(grad_vec, "dp", scatter_dimension=1, tiled=True),
    )
    first_rows, second_cols = (
        lax.all_gather(first_grad, "dp", axis=0, tiled=True),
        lax.all_gather(second_grad, "dp", axis=1, tiled=True),
    )
    first_total, second_total = (
        lax.all_gather(first_rows, "mp", axis=1, tiled=True),
        lax.all_gather(second_cols, "mp", axis=0, tiled=True),
    )
    owned = first_grad.shape[0]
    width = first_grad.shape[1]
    start_dp = lax.axis_index("dp") * owned
    start_mp = lax.axis_index("mp") * width
    left_rows = lax.dynamic_slice_in_dim(first_total, start_dp, owned, 0)
    right_rows = lax.dynamic_slice_in_dim(first_total, start_mp, width, 0)
    left_cols = lax.dynamic_slice_in_dim(first_total, start_dp, owned, 1)
    right_cols = lax.dynamic_slice_in_dim(first_total, start_mp, width, 1)
    first_left_new = stat_decay * first_left + (1.0 - stat_decay) * lax.dot_general(
        left_rows, right_rows, over_cols, precision=high
    )
    first_right_new = stat_decay * first_right + (1.0 - stat_decay) * lax.dot_general(
        left_cols, right_cols, over_rows, precision=high
    )
    first_step = lax.dot_general(
        jnp.dot(first_left_root, first_total, precision=high),
        first_right_root,
        over_cols,
        precision=high,
    )
    first_new = first_weight - shampoo_rate * first_step
    upper_rows = lax.dynamic_slice_in_dim(second_total, start_mp, width, 0)
    lower_rows = lax.dynamic_slice_in_dim(second_total, start_dp, owned, 0)
    upper_cols = lax.dynamic_slice_in_dim(second_total, start_mp, width, 1)
    lower_cols = lax.dynamic_slice_in_dim(second_total, start_dp, owned, 1)
    second_left_new = stat_decay * second_left + (1.0 - stat_decay) * lax.dot_general(
        upper_rows, lower_rows, over_cols, precision=high
    )
    second_right_new = stat_decay * second_right + (1.0 - stat_decay) * lax.dot_general(
        upper_cols, lower_cols, over_rows, precision=high
    )
    second_step = lax.dot_general(
        jnp.dot(second_left_root, second_total, precision=high),
        second_right_root,
        over_cols,
        precision=high,
    )
    second_new = second_weight - shampoo_rate * second_step
    moment_one = beta_first * first_moment + (1.0 - beta_first) * vec_grad
    moment_two = beta_second * second_moment + (1.0 - beta_second) * vec_grad * vec_grad
    corr_one = 1.0 - beta_first**STEP
    corr_two = 1.0 - beta_second**STEP
    members_new = members - adam_rate * (moment_one / corr_one) / (
        jnp.sqrt(moment_two / corr_two) + adam_eps
    )
    return (
        logits,
        input_grad,
        rms_stats,
        first_grad,
        first_new,
        first_left_new,
        first_right_new,
        second_grad,
        second_new,
        second_left_new,
        second_right_new,
        moment_one,
        moment_two,
        members_new,
    )


def solution(mesh):
    placed = (
        P("mp", "dp"),
        P("mp", "dp"),
        P("dp", None),
        P(None, "dp", "mp"),
        P(None, "dp", "mp"),
        P(None, "dp", "mp"),
        P("dp", "mp"),
        P("mp", "dp"),
        P("dp", "mp"),
        P("dp", "mp"),
        P("mp", "dp"),
        P("mp", "dp"),
        P("dp", None),
        P("mp", None),
        P("mp", None),
        P("dp", None),
    )
    return jax.shard_map(
        on_device,
        mesh=mesh,
        in_specs=placed,
        out_specs=(
            P("mp", "dp"),
            P("mp", "dp"),
            P(),
            P("dp", "mp"),
            P("dp", "mp"),
            P("dp", "mp"),
            P("dp", "mp"),
            P("mp", "dp"),
            P("mp", "dp"),
            P("mp", "dp"),
            P("mp", "dp"),
            P(None, "dp", "mp"),
            P(None, "dp", "mp"),
            P(None, "dp", "mp"),
        ),
        check_vma=False,
    )
```

profile of v0, /device:TPU:0, one launch (start us, length us, event | category | flops | bytes accessed | tf_op | source)
XLA Modules:
  0.0 1112.2 jit_solution(12044640973617156003)
XLA Ops:
  8.9 10.7 all_gather.27
  19.7 3.2 copy.41
  25.2 4.1 copy.39
  29.3 3.4 fusion.14
  32.8 9.2 all_gather.30
  42.0 8.2 all_gather.29
  50.2 124.6 %all-gather.7.cloned.1.call-done = bf16[512,8192]{0,1:T(8,128)(2,1)} async-done(((bf16[128,8192]{0,1:T(8,128)(2,1)}), bf16[512,8192]{0,1:T(8,128)(2,1)}) %all-gather.7.cloned.1.call-update) | async-done | bytes 8388624 | tf_op jit(solution)/shard_map/all_gather | solution.py:150
  174.8 7.8 convolution_bitcast_fusion.2
  182.6 141.2 %all-gather.5.cloned.1.call-done = bf16[512,8192]{0,1:T(8,128)(2,1)} async-done(((bf16[128,8192]{0,1:T(8,128)(2,1)}), bf16[512,8192]{0,1:T(8,128)(2,1)}) %all-gather.5.cloned.1.call-update) | async-done | bytes 8388624 | tf_op jit(solution)/shard_map/all_gather | solution.py:129
  323.8 10.1 fusion.42
  333.9 4.1 fusion.47
  338.2 2.4 fusion.10
  341.9 6.5 fusion.45
  348.5 21.4 %reduce-scatter.12.cloned.1.call-done = f32[128,64]{0,1:T(8,128)} async-done(((f32[128,512]{0,1:T(8,128)}), f32[128,64]{0,1:T(8,128)}) %reduce-scatter.12.cloned.1.call-update) | async-done | bytes 32784 | tf_op jit(solution)/shard_map/reduce_scatter | solution.py:171
  369.9 10.2 all_gather.34
  380.2 27.1 %reduce-scatter.10.cloned.1.call-done = f32[64,128]{1,0:T(8,128)} async-done(((f32[512,128]{1,0:T(8,128)}), f32[64,128]{1,0:T(8,128)}) %reduce-scatter.10.cloned.1.call-update) | async-done | bytes 32784 | tf_op jit(solution)/shard_map/reduce_scatter | solution.py:170
  407.3 10.2 all_gather.32
  417.6 9.7 convolution_bitcast_fusion
  427.3 8.1 convolution_bitcast_fusion.1
  438.5 2.4 reduce_sum.140
  441.0 2.4 reduce_sum.144
  443.4 2.6 reduce_sum.142
  446.1 2.4 fusion.19
  450.6 18.3 %all-gather.9.cloned.1.call-done = f32[512,512]{1,0:T(8,128)} async-done(((f32[512,128]{1,0:T(8,128)}), f32[512,512]{1,0:T(8,128)}) %all-gather.9.cloned.1.call-update) | async-done | bytes 1048592 | tf_op jit(solution)/shard_map/all_gather | solution.py:179
  479.4 270.4 %reduce-scatter.8.cloned.1.call-done = f32[128,8192]{0,1:T(8,128)} async-done(((f32[512,8192]{0,1:T(8,128)}), f32[128,8192]{0,1:T(8,128)}) %reduce-scatter.8.cloned.1.call-update) | async-done | bytes 4194320 | tf_op jit(solution)/shard_map/reduce_scatter | solution.py:163
  749.9 283.6 %reduce-scatter.6.cloned.1.call-done = f32[128,8192]{0,1:T(8,128)} async-done(((f32[512,8192]{0,1:T(8,128)}), f32[128,8192]{0,1:T(8,128)}) %reduce-scatter.6.cloned.1.call-update) | async-done | bytes 4194320 | tf_op jit(solution)/shard_map/reduce_scatter | solution.py:133
  1033.4 10.3 convert_multiply_fusion
  1046.2 2.4 reduce_sum.146
  1048.6 2.6 reduce_sum.148
  1051.9 41.4 %all-reduce.1 = (f32[1]{0:T(128)}, f32[1]{0:T(128)}, f32[]{:T(128)}) all-reduce(f32[1]{0:T(128)} %bitcast.29, f32[1]{0:T(128)} %bitcast.28, f32[]{:T(128)S(6)} %mul.263), channel_id=1, replica_groups=mesh['dp'=8,'mp'=4] {'dp','mp'}, use_global_device_ids=true, to_apply=%region_5.0 | all-reduce | flops 3 | bytes 24 | tf_op jit(solution)/shard_map/psum | solution.py:137
  1095.9 4.1 copy.44
  1100.0 2.9 copy.43
  (100 shorter events, 28.2 us)
Async XLA Ops:
  7.2 466.1 %copy-start = (f32[128,512]{1,0:T(8,128)S(1)}, f32[128,512]{1,0:T(8,128)}, u32[]{:S(2)}) copy-start(f32[128,512]{1,0:T(8,128)} %param.30) | copy-start | bytes 786436
  7.2 167.6 %all-gather.7.cloned.1.call-start = ((), (), s32[]{:S(2)}) async-start(), calls=%async_computation.6 | async-start | bytes 10485760 | tf_op jit(solution)/shard_map/all_gather | solution.py:150
  22.9 6.4 copy-start.2
  25.2 298.5 %all-gather.5.cloned.1.call-start = ((), (), s32[]{:S(2)}) async-start(), calls=%async_computation.4 | async-start | bytes 10485760 | tf_op jit(solution)/shard_map/all_gather | solution.py:129
  29.3 3.5 copy-start.9
  29.3 3.5 copy-start.8
  32.7 337.2 %reduce-scatter.12.cloned.1.call-start = ((), (), s32[]{:S(2)}) async-start(), calls=%async_computation.10 | async-start | bytes 294912 | tf_op jit(solution)/shard_map/reduce_scatter | solution.py:171
  323.7 10.1 copy-start.1
  338.0 69.3 %reduce-scatter.10.cloned.1.call-start = ((), (), s32[]{:S(2)}) async-start(), calls=%async_computation.8 | async-start | bytes 294912 | tf_op jit(solution)/shard_map/reduce_scatter | solution.py:170
  340.6 1.3 copy-start.4
  348.5 97.7 %all-gather.11.cloned.1.call-start = ((), (), s32[]{:S(2)}) async-start(), calls=%async_computation.11 | async-start | bytes 1310720 | tf_op jit(solution)/shard_map/all_gather | solution.py:180
  380.2 88.7 %all-gather.9.cloned.1.call-start = ((), (), s32[]{:S(2)}) async-start(), calls=%async_computation.9 | async-start | bytes 1310720 | tf_op jit(solution)/shard_map/all_gather | solution.py:179
  417.5 332.4 %reduce-scatter.8.cloned.1.call-start = ((), (), s32[]{:S(2)}) async-start(), calls=%async_computation.7 | async-start | bytes 20971520 | tf_op jit(solution)/shard_map/reduce_scatter | solution.py:163
  427.2 606.2 %reduce-scatter.6.cloned.1.call-start = ((), (), s32[]{:S(2)}) async-start(), calls=%async_computation.5 | async-start | bytes 20971520 | tf_op jit(solution)/shard_map/reduce_scatter | solution.py:133
  435.3 0.7 copy-start.20
  435.3 1.9 copy-start.12
  435.4 668.9 %all-reduce.4.cloned.1.call-start = ((), (), s32[]{:S(2)}) async-start(), calls=%async_computation.12 | async-start | bytes 196608
  440.9 5.2 copy-start.16
  440.9 7.6 copy-start.14
  440.9 27.9 %copy-start.15 = (f32[64,128]{1,0:T(8,128)S(1)}, f32[64,128]{1,0:T(8,128)}, u32[]{:S(2)}) copy-start(f32[64,128]{1,0:T(8,128)} %param.24) | copy-start | bytes 98308
  441.0 30.0 %copy-start.17 = (f32[64,128]{1,0:T(8,128)S(1)}, f32[64,128]{1,0:T(8,128)}, u32[]{:S(2)}) copy-start(f32[64,128]{1,0:T(8,128)} %param.25) | copy-start | bytes 98308
  443.4 32.1 %copy-start.10 = (f32[64,512]{1,0:T(8,128)S(1)}, f32[64,512]{1,0:T(8,128)}, u32[]{:S(2)}) copy-start(f32[64,512]{1,0:T(8,128)} %param.31) | copy-start | bytes 393220
  443.4 33.0 %copy-start.11 = (f32[64,512]{1,0:T(8,128)S(1)}, f32[64,512]{1,0:T(8,128)}, u32[]{:S(2)}) copy-start(f32[64,512]{1,0:T(8,128)} %param.28) | copy-start | bytes 393220
  443.4 35.0 %copy-start.6 = (f32[128,512]{1,0:T(8,128)S(1)}, f32[128,512]{1,0:T(8,128)}, u32[]{:S(2)}) copy-start(f32[128,512]{1,0:T(8,128)} %param.29) | copy-start | bytes 786436
  443.4 590.0 %copy-start.3 = (bf16[128,8192]{0,1:T(8,128)(2,1)S(1)}, bf16[128,8192]{0,1:T(8,128)(2,1)}, u32[]{:S(2)}) copy-start(bf16[128,8192]{0,1:T(8,128)(2,1)} %copy-done.2) | copy-start | bytes 6291460
  1048.6 51.3 %copy-start.5 = (bf16[128,8192]{0,1:T(8,128)(2,1)S(1)}, bf16[128,8192]{0,1:T(8,128)(2,1)}, u32[]{:S(2)}) copy-start(bf16[128,8192]{0,1:T(8,128)(2,1)} %get-tuple-element.73) | copy-start | bytes 6291460
  1051.3 0.6 copy-start.7
  1095.8 8.4 copy-start.13
  1095.8 8.4 copy-start.18
  1095.8 8.4 copy-start.19
Sparse Core Ops, SparseCore 0:
  25.3 149.4 all-gather.6
  176.4 147.3 all-gather.4
  338.1 31.7 reduce-scatter.11
  373.7 33.5 reduce-scatter.9
  408.7 30.1 all-gather.10
  440.3 28.4 all-gather.8
  471.2 278.5 reduce-scatter.7
  752.3 281.0 reduce-scatter.5
  1052.0 52.1 all-reduce.3
where the time goes:
time: 1110 us
  waiting for transfers between devices  888 us (80%)
  blocking collectives  89.9 us (8%)
  matrix products  61.1 us (6%)
  other arithmetic  37.9 us (3%)
  local copies, waits for them, and re-layouts  18.3 us (2%)
  between operations  16.2 us (1%)
    reduce_scatter x1, waiting for transfers between devices, on_device(): lax.psum_scatter(partial_value, 'mp', scatter_dimension=0, tiled=True)  284 us
    reduce_scatter x1, waiting for transfers between devices, on_device(): lax.psum_scatter(partial_back, 'mp', scatter_dimension=0, tiled=True)  270 us
    all_gather x1, waiting for transfers between devices, on_device(): gathered = lax.all_gather(scaled, 'mp', axis=0, tiled=True)  141 us
    all_gather x1, waiting for transfers between devices, on_device(): grad_full = lax.all_gather(grad_proj, 'mp', axis=0, tiled=True)  125 us
    psum x1, blocking collectives, on_device(): lax.psum((jnp.sum(weight_mask * values * values), jnp.sum(weight_mask * b...  41.4 us
    reduce_scatter x1, waiting for transfers between devices, on_device(): lax.psum_scatter(grad_first, 'dp', scatter_dimension=0, tiled=True)  27.1 us
  transfers between devices with their start and end apart: 9, of which 8 were waited for; matrix products, arithmetic and copies ran while one was open for 7% of the time, Pallas kernels for 0%

commit v1 on v0

v1 whole, which is shorter than its diff:
```python
import functools

import jax
import jax.numpy as jnp
from jax import lax
from jax.experimental import pallas as pl
from jax.experimental.pallas import tpu as pltpu
from jax.sharding import PartitionSpec as P

K = 32
STEP = 10
LANES = 128
CHUNK = 256
ROWS = 32
AHEAD = 2

beta_first = 0.9
beta_second = 0.999
adam_eps = 1e-08
adam_rate = 0.2
stat_decay = 0.95
shampoo_rate = 1.0
curve_a = 0.7978845608028654
curve_b = 0.044715

MESH = pl.DeviceIdType.MESH
F32 = jnp.float32
BF16 = jnp.bfloat16
over_lanes = (((1,), (1,)), ((), ()))


def flip(index, mask):
    bit = 1
    while bit <= mask:
        if mask & bit:
            index = index + bit - 2 * bit * ((index // bit) % 2)
        bit *= 2
    return index


def mm(a, b):
    return jnp.dot(a, b, preferred_element_type=F32)


def mm_t(a, b, precision=None):
    return lax.dot_general(a, b, over_lanes, precision=precision, preferred_element_type=F32)


def multiple(value, by):
    return pl.multiple_of(value, by)


def kernel(
    N,
    M,
    x_hbm,
    cot_hbm,
    mask_hbm,
    mem_hbm,
    m1_hbm,
    m2_hbm,
    w1_hbm,
    w2_hbm,
    l1_hbm,
    r1_hbm,
    l2_hbm,
    r2_hbm,
    p1_hbm,
    q1_hbm,
    p2_hbm,
    q2_hbm,
    logits_hbm,
    igrad_hbm,
    rms_ref,
    g1_out,
    w1_out,
    l1_out,
    r1_out,
    g2_out,
    w2_out,
    l2_out,
    r2_out,
    m1_out,
    m2_out,
    mem_out,
    mask_v,
    mem_v,
    m1_v,
    m2_v,
    w1_v,
    w2_v,
    l1_v,
    r1_v,
    l2_v,
    r2_v,
    p1_v,
    q1_v,
    p2_v,
    q2_v,
    xb,
    cb,
    lgb,
    igb,
    wb,
    tb,
    w1,
    w1t,
    w2,
    w2t,
    tab,
    stage,
    mk,
    hp,
    hid,
    dgm,
    prod,
    sc,
    hi,
    gp,
    gpre,
    g1,
    g2t,
    vec,
    vt,
    stat,
    gb,
    rcore,
    rxy,
    rz,
    ga,
    g1f,
    g1ft,
    g2f,
    g2ft,
    local_sem,
    in_send,
    x_recv,
    c_recv,
    own_sem,
    out_send,
    out_own,
    out_recv,
    wz_send,
    wz_recv,
    wx_send,
    wx_recv,
    wc_send,
    wc_recv,
    gc_send,
    gc_recv,
    gx_send,
    gx_recv,
    gz_send,
    gz_recv,
    az_send,
    az_recv,
    ax_send,
    ax_recv,
    ac_send,
    ac_recv,
):
    F, R = x_hbm.shape
    D = F * M
    Q = N // 2
    mine = R // M
    w = min(CHUNK, mine)
    C = mine // w
    tiles = w // LANES
    kb = K // N
    dr = D // N
    tr = tb.shape[3]
    pr = gb.shape[3]
    blocks = D // ROWS
    high = lax.Precision.HIGHEST

    d, m = lax.axis_index("dp"), lax.axis_index("mp")
    c, q = d % 2, d // 2

    def z_peer(o):
        return (d, flip(m, o))

    def xy_peer(o):
        return (flip(q, o) * 2 + c, m)

    core_peer = (flip(d, 1), m)
    z_order = sorted(range(1, M), reverse=True)
    xy_order = sorted(range(1, Q), reverse=True)

    def remote(src, dst, send, recv, peer):
        return pltpu.make_async_remote_copy(
            src_ref=src, dst_ref=dst, send_sem=send, recv_sem=recv, device_id=peer, device_id_type=MESH
        )

    pairs = (
        (mask_hbm, mask_v),
        (mem_hbm, mem_v),
        (w1_hbm, w1_v),
        (w2_hbm, w2_v),
        (m1_hbm, m1_v),
        (m2_hbm, m2_v),
        (l1_hbm, l1_v),
        (r1_hbm, r1_v),
        (l2_hbm, l2_v),
        (r2_hbm, r2_v),
        (p1_hbm, p1_v),
        (q1_hbm, q1_v),
        (p2_hbm, p2_v),
        (q2_hbm, q2_v),
    )
    loads = [pltpu.make_async_copy(a, b, local_sem.at[i]) for i, (a, b) in enumerate(pairs)]
    for load in loads:
        load.start()

    with jax.named_scope("barrier"):
        entry = pltpu.get_barrier_semaphore()
        peers = [z_peer(o) for o in z_order] + [xy_peer(o) for o in xy_order] + [core_peer]
        for peer in peers:
            pl.semaphore_signal(entry, inc=1, device_id=peer, device_id_type=MESH)
        pl.semaphore_wait(entry, len(peers))

    def send_in(i):
        col = multiple(i * w, w)
        here = pl.ds(multiple(m * F, F), F)
        for hbm, buf, sem in ((x_hbm, xb, x_recv), (cot_hbm, cb, c_recv)):
            for o in z_order:
                to = flip(m, o)
                remote(
                    hbm.at[:, pl.ds(multiple(to * mine + i * w, w), w)],
                    buf.at[here, pl.ds(col, w)],
                    in_send,
                    sem.at[i],
                    (d, to),
                ).start()
        for hbm, buf, sem in ((x_hbm, xb, own_sem.at[0, i]), (cot_hbm, cb, own_sem.at[1, i])):
            pltpu.make_async_copy(
                hbm.at[:, pl.ds(multiple(m * mine + i * w, w), w)], buf.at[here, pl.ds(col, w)], sem
            ).start()

    others = (M - 1) * F

    def wait_in(i):
        for hbm, buf, sem, own in ((x_hbm, xb, x_recv, own_sem.at[0, i]), (cot_hbm, cb, c_recv, own_sem.at[1, i])):
            part = buf.at[pl.ds(0, others), pl.ds(0, w)]
            remote(part, part, in_send, sem.at[i], z_peer(1)).wait_recv()
            block = buf.at[pl.ds(0, F), pl.ds(0, w)]
            pltpu.make_async_copy(hbm.at[:, pl.ds(0, w)], block, own).wait()

    def send_out(kind, i):
        buf, hbm = ((lgb, logits_hbm), (igb, igrad_hbm))[kind]
        col = multiple(i * w, w)
        there = pl.ds(multiple(m * mine + i * w, w), w)
        for o in z_order:
            to = flip(m, o)
            remote(
                buf.at[pl.ds(multiple(to * F, F), F), pl.ds(col, w)],
                hbm.at[:, there],
                out_send.at[kind, i],
                out_recv.at[kind],
                (d, to),
            ).start()
        pltpu.make_async_copy(
            buf.at[pl.ds(multiple(m * F, F), F), pl.ds(col, w)], hbm.at[:, there], out_own.at[kind, i]
        ).start()

    def wait_out(kind, i):
        buf, hbm = ((lgb, logits_hbm), (igb, igrad_hbm))[kind]
        part = buf.at[pl.ds(0, others), pl.ds(0, w)]
        remote(part, part, out_send.at[kind, i], out_recv.at[kind], z_peer(1)).wait_send()
        pltpu.make_async_copy(buf.at[pl.ds(0, F), pl.ds(0, w)], hbm.at[:, pl.ds(0, w)], out_own.at[kind, i]).wait()

    for load in loads[:4]:
        load.wait()
    wb[c, q, m, 0:dr, :] = w1_v[...].astype(BF16)
    wb[c, q, m, dr : 2 * dr, :] = w2_v[...].T.astype(BF16)
    for t in range(6):
        tb[c, q, m, t * kb : (t + 1) * kb, :] = mem_v[t]

    bufs = (wb, tb)
    for o in z_order:
        for k, buf in enumerate(bufs):
            remote(buf.at[c, q, m], buf.at[c, q, m], wz_send.at[k, o], wz_recv.at[k, o], z_peer(o)).start()
    for i in range(min(AHEAD, C)):
        send_in(i)

    per_mask = LANES // K
    groups = mine // LANES
    start = multiple(m * groups * per_mask, groups * per_mask)
    mk[...] = jnp.concatenate(
        [mask_v[pl.ds(start + j, groups, stride=per_mask), :] for j in range(per_mask)], axis=1
    ).astype(F32)

    def clear(i, carry):
        rows = pl.ds(multiple(i * ROWS, ROWS), ROWS)
        g1[rows, :] = jnp.zeros((ROWS, D), F32)
        g2t[rows, :] = jnp.zeros((ROWS, D), F32)
        for t in range(6):
            vec[t, rows, :] = jnp.zeros((ROWS, LANES), F32)
        return carry

    lax.fori_loop(0, blocks, clear, 0)
    stat[...] = jnp.zeros_like(stat)

    with jax.named_scope("weights_z"):
        for o in z_order:
            for k, buf in enumerate(bufs):
                remote(buf.at[c, q, m], buf.at[c, q, flip(m, o)], wz_send.at[k, o], wz_recv.at[k, o], z_peer(o)).wait()
    with jax.named_scope("weights_xy"):
        for o in xy_order:
            for k, buf in enumerate(bufs):
                remote(buf.at[c, q], buf.at[c, q], wx_send.at[k, o], wx_recv.at[k, o], xy_peer(o)).start()
        for o in xy_order:
            for k, buf in enumerate(bufs):
                remote(buf.at[c, q], buf.at[c, flip(q, o)], wx_send.at[k, o], wx_recv.at[k, o], xy_peer(o)).wait()
    with jax.named_scope("weights_core"):
        for k, buf in enumerate(bufs):
            remote(buf.at[c], buf.at[c], wc_send.at[k], wc_recv.at[k], core_peer).start()
        for k, buf in enumerate(bufs):
            remote(buf.at[c], buf.at[1 - c], wc_send.at[k], wc_recv.at[k], core_peer).wait()

    with jax.named_scope("weights_spread"):

        def place(i, carry):
            rows = pl.ds(multiple(i * dr, dr), dr)
            for j in range(M):
                cols = slice(j * F, (j + 1) * F)
                w1[rows, cols] = wb[i % 2, i // 2, j, 0:dr, :]
                w2t[rows, cols] = wb[i % 2, i // 2, j, dr : 2 * dr, :]
            return carry

        lax.fori_loop(0, N, place, 0)

        def turn(i, carry):
            here = pl.ds(multiple(i * LANES, LANES), LANES)
            for j in range(D // LANES):
                there = slice(j * LANES, (j + 1) * LANES)
                w1t[there, here] = w1[here, there].astype(F32).T.astype(BF16)
                w2[there, here] = w2t[here, there].astype(F32).T.astype(BF16)
            return carry

        lax.fori_loop(0, D // LANES, turn, 0)
        for t in range(6):
            for i in range(N):
                for j in range(M):
                    stage[t, i * kb : (i + 1) * kb, j * F : (j + 1) * F] = tb[
                        i % 2, i // 2, j, t * kb : (t + 1) * kb, :
                    ]

        def table(t, carry):
            for j in range(D // LANES):
                cols = slice(j * LANES, (j + 1) * LANES)
                piece = stage[t, :, cols]
                tab[t, cols, :] = jnp.concatenate([piece] * per_mask, axis=0).T
            return carry

        lax.fori_loop(0, 6, table, 0)

    def eight(value):
        return value.reshape(ROWS // 8, 8, LANES).sum(0)

    def work(i, carry):
        col = multiple(i * w, w)
        with jax.named_scope("wait_in"):
            wait_in(i)

        @pl.when(i + AHEAD < C)
        def _():
            send_in(i + AHEAD)

        first_out = max(C - 2, 0)

        @pl.when(i >= first_out)
        def _():
            for kind in range(2):
                send_out(kind, i - first_out)

        masks = [mk[pl.ds(i * tiles + j, 1), :] for j in range(tiles)]

        def place_of(r):
            return pl.ds(multiple(r * ROWS, ROWS), ROWS)

        def lanes_of(j):
            return pl.ds(multiple(col + j * LANES, LANES), LANES)

        def scale_rows(r, sums):
            rows = place_of(r)
            row_in = tab[0, rows, :]
            new = []
            for j in range(tiles):
                x = xb[rows, lanes_of(j)].astype(F32)
                sc[rows, j * LANES : (j + 1) * LANES] = (x * row_in).astype(BF16)
                new.append(sums[j] + eight(x * x))
            return tuple(new)

        zero = tuple(jnp.zeros((8, LANES), F32) for _ in range(tiles))
        with jax.named_scope("scale"):
            x_sums = lax.fori_loop(0, blocks, scale_rows, zero)
        with jax.named_scope("mm_one"):
            hp[...] = mm(w1t[...], sc[...])

        def curve_rows(r, carry):
            rows = place_of(r)
            gain, bias, row_mid = tab[1, rows, :], tab[2, rows, :], tab[3, rows, :]
            for j in range(tiles):
                cols = slice(j * LANES, (j + 1) * LANES)
                s = hp[rows, cols] * gain + bias
                s2 = s * s
                th = jnp.tanh(curve_a * (s + curve_b * (s2 * s)))
                cdf = 0.5 * (1.0 + th)
                h = s * cdf
                slope = cdf + (0.5 * s) * (1.0 - th * th) * (curve_a + (3.0 * curve_a * curve_b) * s2)
                hid[rows, cols] = h
                dgm[rows, cols] = slope * row_mid
                hi[rows, cols] = (h * row_mid).astype(BF16)
            return carry

        with jax.named_scope("curve"):
            lax.fori_loop(0, blocks, curve_rows, 0)
        with jax.named_scope("mm_two"):
            prod[...] = mm(w2t[...], hi[...])

        def out_rows(r, sums):
            rows = place_of(r)
            gain, bias = tab[4, rows, :], tab[5, rows, :]
            v4, v5 = vec[4, rows, :], vec[5, rows, :]
            new = []
            for j in range(tiles):
                cols = slice(j * LANES, (j + 1) * LANES)
                x = xb[rows, lanes_of(j)].astype(F32)
                projected = prod[rows, cols]
                branch = projected * gain + bias
                lgb[rows, lanes_of(j)] = (x + branch).astype(BF16)
                new.append(sums[j] + eight(branch * branch))
                go = cb[rows, lanes_of(j)].astype(F32) * masks[j]
                v5 = v5 + go
                v4 = v4 + go * projected
                gp[rows, cols] = (go * gain).astype(BF16)
            vec[4, rows, :] = v4
            vec[5, rows, :] = v5
            return tuple(new)

        with jax.named_scope("out"):
            b_sums = lax.fori_loop(0, blocks, out_rows, zero)
        for j in range(tiles):
            stat[0:8, :] += x_sums[j] * masks[j]
            stat[8:16, :] += b_sums[j] * masks[j]

        with jax.named_scope("mm_three"):
            half = D // 2
            for k in range(2):
                part = slice(k * half, (k + 1) * half)
                g2t[part, :] += mm_t(gp[part, :], hi[...])
            prod[...] = mm(w2[...], gp[...])

        def back_rows(r, carry):
            rows = place_of(r)
            gain = tab[1, rows, :]
            v1, v2, v3 = vec[1, rows, :], vec[2, rows, :], vec[3, rows, :]
            for j in range(tiles):
                cols = slice(j * LANES, (j + 1) * LANES)
                gh = prod[rows, cols]
                v3 = v3 + gh * hid[rows, cols]
                gs = gh * dgm[rows, cols]
                v2 = v2 + gs
                v1 = v1 + gs * hp[rows, cols]
                gpre[rows, cols] = (gs * gain).astype(BF16)
            vec[1, rows, :] = v1
            vec[2, rows, :] = v2
            vec[3, rows, :] = v3
            return carry

        with jax.named_scope("back"):
            lax.fori_loop(0, blocks, back_rows, 0)
        with jax.named_scope("mm_four"):
            for k in range(2):
                part = slice(k * half, (k + 1) * half)
                g1[part, :] += mm_t(sc[part, :], gpre[...])
            prod[...] = mm(w1[...], gpre[...])

        def in_rows(r, carry):
            rows = place_of(r)
            row_in = tab[0, rows, :]
            v0 = vec[0, rows, :]
            for j in range(tiles):
                cols = slice(j * LANES, (j + 1) * LANES)
                gs = prod[rows, cols]
                v0 = v0 + gs * xb[rows, lanes_of(j)].astype(F32)
                go = cb[rows, lanes_of(j)].astype(F32) * masks[j]
                igb[rows, lanes_of(j)] = (gs * row_in + go).astype(BF16)
            vec[0, rows, :] = v0
            return carry

        with jax.named_scope("in"):
            lax.fori_loop(0, blocks, in_rows, 0)
        return carry

    lax.fori_loop(0, C, work, 0)

    items = [(kind, i) for i in range(C) for kind in range(2)]
    already = 2 * min(C, 2)
    state = {"sent": already, "done": 0}

    def pump(count=1):
        with jax.named_scope("pump"):
            for _ in range(count):
                if state["sent"] < len(items):
                    wait_out(*items[state["done"]])
                    state["done"] += 1
                    send_out(*items[state["sent"]])
                    state["sent"] += 1

    with jax.named_scope("pack"):

        def pack_g(i, carry):
            rows = pl.ds(multiple(i * dr, dr), dr)
            for j in range(M):
                cols = slice(j * F, (j + 1) * F)
                gb[i % 2, i // 2, j, 0:dr, :] = g1[rows, cols]
                gb[i % 2, i // 2, j, dr : 2 * dr, :] = g2t[rows, cols]
            return carry

        lax.fori_loop(0, N, pack_g, 0)

        def fold(t, carry):
            for j in range(D // LANES):
                cols = slice(j * LANES, (j + 1) * LANES)
                turned = vec[t, cols, :].T
                vt[t, :, cols] = sum(turned[k * K : (k + 1) * K, :] for k in range(per_mask))
            return carry

        lax.fori_loop(0, 6, fold, 0)
        for t in range(6):
            for i in range(N):
                for j in range(M):
                    row = 2 * dr + t * kb
                    gb[i % 2, i // 2, j, row : row + kb, :] = vt[t, i * kb : (i + 1) * kb, j * F : (j + 1) * F]
        totals = [stat[0:8, :], stat[8:16, :], jnp.pad(mk[...], ((0, -groups % 8), (0, 0)))]
        rows8 = [jnp.sum(v, keepdims=True).reshape(1, 1) for v in totals]
        row_id = lax.broadcasted_iota(jnp.int32, (8, F), 0)
        lines = sum(jnp.where(row_id == k, v, 0.0) for k, v in enumerate(rows8))

        def put(i, carry):
            for j in range(M):
                gb[i % 2, i // 2, j, 2 * dr + tr : pr, :] = lines
            return carry

        lax.fori_loop(0, N, put, 0)

    pump()
    with jax.named_scope("sum_core"):
        for o in xy_order + [0]:
            k = flip(q, o)
            remote(gb.at[1 - c, k], rcore.at[k], gc_send.at[o], gc_recv.at[o], core_peer).start()

        def add_core(k):
            def step(j, carry):
                gb[c, k, j] += rcore[k, j]
                return carry

            lax.fori_loop(0, M, step, 0)

        for o in xy_order + [0]:
            k = flip(q, o)
            remote(gb.at[1 - c, k], rcore.at[k], gc_send.at[o], gc_recv.at[o], core_peer).wait()
            add_core(k)
            if o:
                remote(gb.at[c, k], rxy.at[o], gx_send.at[o], gx_recv.at[o], xy_peer(o)).start()
    pump(2)
    with jax.named_scope("sum_xy"):
        for o in xy_order:
            k = flip(q, o)
            remote(gb.at[c, k], rxy.at[o], gx_send.at[o], gx_recv.at[o], xy_peer(o)).wait()

            def step(j, carry):
                gb[c, q, j] += rxy[o, j]
                return carry

            lax.fori_loop(0, M, step, 0)
    with jax.named_scope("sum_z"):
        for o in z_order:
            remote(gb.at[c, q, flip(m, o)], rz.at[o], gz_send.at[o], gz_recv.at[o], z_peer(o)).start()
        pump(2)
        for o in z_order:
            remote(gb.at[c, q, flip(m, o)], rz.at[o], gz_send.at[o], gz_recv.at[o], z_peer(o)).wait()
            gb[c, q, m] += rz[o]

    total = gb[c, q, m]
    ga[c, q, m] = total[0 : 2 * dr, :].astype(BF16)
    with jax.named_scope("spread_z"):
        for o in z_order:
            remote(ga.at[c, q, m], ga.at[c, q, m], az_send.at[o], az_recv.at[o], z_peer(o)).start()
        for load in loads[4:]:
            load.wait()
        g1_out[...] = total[0:dr, :]
        g2_out[...] = total[dr : 2 * dr, :].T
        corr_one = 1.0 - beta_first**STEP
        corr_two = 1.0 - beta_second**STEP
        for t in range(6):
            row = 2 * dr + t * kb
            grad = total[row : row + kb, :]
            one = beta_first * m1_v[t] + (1.0 - beta_first) * grad
            two = beta_second * m2_v[t] + (1.0 - beta_second) * grad * grad
            m1_out[t] = one
            m2_out[t] = two
            mem_out[t] = mem_v[t] - adam_rate * (one / corr_one) / (jnp.sqrt(two / corr_two) + adam_eps)
        row = 2 * dr + tr
        count = total[row + 2 : row + 3, 0:1] * D
        rms_ref[:, 0:1] = jnp.sqrt(total[row : row + 1, 0:1] / count)
        rms_ref[:, 1:2] = jnp.sqrt(total[row + 1 : row + 2, 0:1] / count)
        pump(2)
        for o in z_order:
            remote(ga.at[c, q, m], ga.at[c, q, flip(m, o)], az_send.at[o], az_recv.at[o], z_peer(o)).wait()
    with jax.named_scope("spread_xy"):
        for o in xy_order:
            remote(ga.at[c, q], ga.at[c, q], ax_send.at[o], ax_recv.at[o], xy_peer(o)).start()
        pump(1)
        for o in xy_order:
            remote(ga.at[c, q], ga.at[c, flip(q, o)], ax_send.at[o], ax_recv.at[o], xy_peer(o)).wait()
    with jax.named_scope("spread_core"):
        remote(ga.at[c], ga.at[c], ac_send, ac_recv, core_peer).start()
        remote(ga.at[c], ga.at[1 - c], ac_send, ac_recv, core_peer).wait()
    pump(1)

    with jax.named_scope("shampoo"):

        def place_g(i, carry):
            rows = pl.ds(multiple(i * dr, dr), dr)
            for j in range(M):
                cols = slice(j * F, (j + 1) * F)
                g1f[rows, cols] = ga[i % 2, i // 2, j, 0:dr, :]
                g2ft[rows, cols] = ga[i % 2, i // 2, j, dr : 2 * dr, :]
            return carry

        lax.fori_loop(0, N, place_g, 0)

        def turn_g(i, carry):
            here = pl.ds(multiple(i * LANES, LANES), LANES)
            for j in range(D // LANES):
                there = slice(j * LANES, (j + 1) * LANES)
                g1ft[there, here] = g1f[here, there].astype(F32).T.astype(BF16)
                g2f[there, here] = g2ft[here, there].astype(F32).T.astype(BF16)
            return carry

        lax.fori_loop(0, D // LANES, turn_g, 0)
        by_d = pl.ds(multiple(d * dr, dr), dr)
        by_m = pl.ds(multiple(m * F, F), F)

        def renewed(old, fresh):
            return stat_decay * old + (1.0 - stat_decay) * fresh

        l1_out[...] = renewed(l1_v[...], mm_t(g1f[by_d, :], g1f[by_m, :]))
        r1_out[...] = renewed(r1_v[...], mm_t(g1ft[by_d, :], g1ft[by_m, :]))
        l2_out[...] = renewed(l2_v[...], mm_t(g2f[by_m, :], g2f[by_d, :]))
        r2_out[...] = renewed(r2_v[...], mm_t(g2ft[by_m, :], g2ft[by_d, :]))

        def stepped(weight, left, grad_t, right):
            first = mm_t(left[...], grad_t[...].astype(F32), high)
            return weight[...] - shampoo_rate * mm_t(first, right[...], high)

        w1_out[...] = stepped(w1_v, p1_v, g1ft, q1_v)
        pump(1)
        w2_out[...] = stepped(w2_v, p2_v, g2ft, q2_v)

    with jax.named_scope("drain"):
        pump(len(items))
        while state["done"] < len(items):
            wait_out(*items[state["done"]])
            state["done"] += 1
        for kind, (buf, hbm) in enumerate(((lgb, logits_hbm), (igb, igrad_hbm))):
            part = hbm.at[:, pl.ds(0, (M - 1) * mine)]
            remote(part, part, in_send, out_recv.at[kind], z_peer(1)).wait_recv()
        for buf in (xb, cb):
            part = buf.at[pl.ds(0, others), pl.ds(0, mine)]
            remote(part, part, in_send, out_recv.at[0], z_peer(1)).wait_send()


def solution(mesh):
    N, M = mesh.shape["dp"], mesh.shape["mp"]
    Q = N // 2

    def on_device(*args):
        x, cot, mask, members, m1, m2, w1, w2, l1, r1, l2, r2, p1, q1, p2, q2 = args
        F, R = x.shape
        D = F * M
        mine = R // M
        w = min(CHUNK, mine)
        C = mine // w
        kb = members.shape[1]
        dr = w1.shape[0]
        tr = -(-6 * kb // 8) * 8
        pr = 2 * dr + tr + 8
        S = jax.ShapeDtypeStruct
        V = pltpu.VMEM
        dma = pltpu.SemaphoreType.DMA
        outs = [S(x.shape, BF16), S(x.shape, BF16), S((1, 2), F32)]
        outs += [S(a.shape, F32) for a in (w1, w1, l1, r1, w2, w2, l2, r2, m1, m2, members)]
        scratch = [V(a.shape, a.dtype) for a in (mask, members, m1, m2, w1, w2, l1, r1, l2, r2, p1, q1, p2, q2)]
        scratch += [V((D, mine), BF16)] * 4
        scratch += [V((2, Q, M, 2 * dr, F), BF16), V((2, Q, M, tr, F), F32)]
        scratch += [V((D, D), BF16)] * 4
        scratch += [V((6, D, LANES), F32), V((6, K, D), F32), V((mine // LANES, LANES), F32)]
        scratch += [V((D, w), F32)] * 4
        scratch += [V((D, w), BF16)] * 4
        scratch += [V((D, D), F32)] * 2
        scratch += [V((6, D, LANES), F32), V((6, K, D), F32), V((16, LANES), F32)]
        scratch += [V((2, Q, M, pr, F), F32), V((Q, M, pr, F), F32), V((Q, M, pr, F), F32), V((M, pr, F), F32)]
        scratch += [V((2, Q, M, 2 * dr, F), BF16)]
        scratch += [V((D, D), BF16)] * 4
        scratch += [dma((14,)), dma, dma((C,)), dma((C,)), dma((2, C)), dma((2, C)), dma((2, C)), dma((2,))]
        scratch += [dma((2, M)), dma((2, M)), dma((2, Q)), dma((2, Q)), dma((2,)), dma((2,))]
        scratch += [dma((Q,)), dma((Q,)), dma((Q,)), dma((Q,)), dma((M,)), dma((M,))]
        scratch += [dma((M,)), dma((M,)), dma((Q,)), dma((Q,)), dma, dma]
        hbm = pl.BlockSpec(memory_space=pl.ANY)
        vmem = pl.BlockSpec(memory_space=pltpu.VMEM)
        res = pl.pallas_call(
            functools.partial(kernel, N, M),
            out_shape=outs,
            in_specs=[hbm] * 16,
            out_specs=[hbm] * 2 + [vmem] * 12,
            scratch_shapes=scratch,
            compiler_params=pltpu.CompilerParams(
                collective_id=0, has_side_effects=True, vmem_limit_bytes=56 << 20
            ),
            name="block",
        )(*args)
        return (res[0], res[1], res[2].reshape(2), *res[3:])

    placed = (
        P("mp", "dp"),
        P("mp", "dp"),
        P("dp", None),
        P(None, "dp", "mp"),
        P(None, "dp", "mp"),
        P(None, "dp", "mp"),
        P("dp", "mp"),
        P("mp", "dp"),
        P("dp", "mp"),
        P("dp", "mp"),
        P("mp", "dp"),
        P("mp", "dp"),
        P("dp", None),
        P("mp", None),
        P("mp", None),
        P("dp", None),
    )
    return jax.shard_map(
        on_device,
        mesh=mesh,
        in_specs=placed,
        out_specs=(
            P("mp", "dp"),
            P("mp", "dp"),
            P(),
            P("dp", "mp"),
            P("dp", "mp"),
            P("dp", "mp"),
            P("dp", "mp"),
            P("mp", "dp"),
            P("mp", "dp"),
            P("mp", "dp"),
            P("mp", "dp"),
            P(None, "dp", "mp"),
            P(None, "dp", "mp"),
            P(None, "dp", "mp"),
        ),
        check_vma=False,
    )
```

time: 1110 us -> 226 us (0.20)
  waiting for transfers between devices: 888 us -> 0 us
  Pallas kernels: 0 us -> 203 us
  blocking collectives: 89.9 us -> 0 us
  matrix products: 61.1 us -> 0 us
  other arithmetic: 37.9 us -> 0 us
  between operations: 16.2 us -> 0.71 us
    reduce_scatter x4 -> x0, waiting for transfers between devices: 602 us -> none  [the longest x1 284 us: on_device(): lax.psum_scatter(partial_value, 'mp', scatter_dimension=0, tiled=True)]
    all_gather x4 -> x0, waiting for transfers between devices: 284 us -> none  [the longest x1 141 us: on_device(): gathered = lax.all_gather(scaled, 'mp', axis=0, tiled=True)]
    pallas_call x0 -> x1, Pallas kernels: none -> 203 us  [on_device(): pl.pallas_call(functools.partial(kernel, N, M), out_shape=outs, in_specs=...]
    dot_general x14 -> x0, matrix products: 61.1 us -> none  [the longest x1 10.1 us: middle_forward(): lax.dot_general(first_low, rows_in, over_rows, preferred_element_type=jnp...]
    all_gather x5 -> x0, blocking collectives: 48.5 us -> none  [the longest x1 10.7 us: on_device(): lax.all_gather(members, 'dp', axis=1, tiled=True)]
    psum x1 -> x0, blocking collectives: 41.4 us -> none  [on_device(): lax.psum((jnp.sum(weight_mask * values * values), jnp.sum(weight_mask * b...]
    reduce_sum x13 -> x0, other arithmetic: 15.5 us -> none  [the longest x6 14.8 us: member_sum(): partial_value = values.reshape(width, -1, repeat * K).sum(1)]
  transfers between devices with their start and end apart: 9 -> 0, of which waited for: 8 -> 0; matrix products, arithmetic and copies ran while one was open for 7% -> 0% of each run, Pallas kernels for 0% -> 0%
where the time goes in v1:
time: 226 us; the launch traced here: 225 us
  Pallas kernels  203 us (90%)
  local copies, waits for them, and re-layouts  21.5 us (10%)
    pallas_call x1, Pallas kernels, on_device(): pl.pallas_call(functools.partial(kernel, N, M), out_shape=outs, in_specs=...  203 us
    unnamed x36, local copies, waits for them, and re-layouts  21.5 us

profile of v1, /device:TPU:0, one launch (start us, length us, event | category | flops | bytes accessed | tf_op | source)
XLA Modules:
  0.0 225.0 jit_solution(15003554844081603570)
XLA Ops:
  0.6 1.5 copy.31.w2_hbm
  2.1 1.5 copy.32.l2_hbm
  3.6 1.5 copy.33.r2_hbm
  5.1 1.5 copy.30.mask_hbm
  6.6 202.8 %block.1 = (bf16[128,8192]{1,0:T(8,128)(2,1)}, bf16[128,8192]{1,0:T(8,128)(2,1)}, f32[1,2]{1,0:T(1,128)}, f32[64,128]{1,0:T(8,128)}, f32[64,128]{1,0:T(8,128)}, ...) custom-call(bf16[128,8192]{1,0:T(8,128)(2,1)} %x_hbm.1, ...), custom_call_target="tpu_custom_call" | custom-call | tf_op jit(solution)/shard_map/block/pallas_call | solution.py:714
  209.4 1.5 copy.34
  210.9 1.5 copy.35
  212.5 1.5 copy.36
  214.0 1.5 copy.37
  215.5 3.2 %copy.48 = bf16[128,8192]{1,0:T(8,128)(2,1)} copy(bf16[128,8192]{1,0:T(8,128)(2,1)} %get-tuple-element.70) | data formatting | bytes 4194304
  218.8 0.0 copy-done
  218.8 0.0 copy-start.2
  218.8 0.0 copy-start.1
  218.8 0.0 copy-start.7
  218.8 0.0 copy-start.6
  218.8 0.0 copy-start.5
  218.9 1.3 copy.49
  220.2 0.0 copy-done.8
  220.2 0.5 copy.50
  220.7 0.0 copy-done.4
  220.7 0.6 copy.51
  221.3 0.0 copy-done.3
  221.3 0.6 copy.52
  221.9 0.0 copy-done.2
  221.9 0.6 copy.53
  222.5 0.0 copy-done.1
  222.5 0.6 copy.54
  223.2 0.0 copy-done.7
  223.2 0.6 copy.55
  223.8 0.0 copy-done.6
  223.8 0.6 copy.56
  224.4 0.6 copy.57
  (5 shorter events, 0.0 us)
Async XLA Ops:
  215.5 3.2 %copy-start = (bf16[128,8192]{1,0:T(8,128)(2,1)S(1)}, bf16[128,8192]{1,0:T(8,128)(2,1)}, u32[]{:S(2)}) copy-start(bf16[128,8192]{1,0:T(8,128)(2,1)} %get-tuple-element.71) | copy-start | bytes 6291460
  218.8 1.4 copy-start.8
  218.8 1.9 copy-start.4
  218.8 2.5 %copy-start.3 = (f32[64,128]{1,0:T(8,128)S(1)}, f32[64,128]{1,0:T(8,128)}, u32[]{:S(2)}) copy-start(f32[64,128]{1,0:T(8,128)} %get-tuple-element.74) | copy-start | bytes 98308
  218.8 3.1 %copy-start.2 = (f32[64,128]{1,0:T(8,128)S(1)}, f32[64,128]{1,0:T(8,128)}, u32[]{:S(2)}) copy-start(f32[64,128]{1,0:T(8,128)} %get-tuple-element.75) | copy-start | bytes 98308
  218.8 3.7 %copy-start.1 = (f32[64,128]{1,0:T(8,128)S(1)}, f32[64,128]{1,0:T(8,128)}, u32[]{:S(2)}) copy-start(f32[64,128]{1,0:T(8,128)} %get-tuple-element.76) | copy-start | bytes 98308
  218.8 4.3 %copy-start.7 = (f32[6,4,128]{2,1,0:T(4,128)S(1)}, f32[6,4,128]{2,1,0:T(4,128)}, u32[]{:S(2)}) copy-start(f32[6,4,128]{2,1,0:T(4,128)} %get-tuple-element.81) | copy-start | bytes 36868
  218.8 4.9 %copy-start.6 = (f32[6,4,128]{2,1,0:T(4,128)S(1)}, f32[6,4,128]{2,1,0:T(4,128)}, u32[]{:S(2)}) copy-start(f32[6,4,128]{2,1,0:T(4,128)} %get-tuple-element.82) | copy-start | bytes 36868
  218.8 5.5 %copy-start.5 = (f32[6,4,128]{2,1,0:T(4,128)S(1)}, f32[6,4,128]{2,1,0:T(4,128)}, u32[]{:S(2)}) copy-start(f32[6,4,128]{2,1,0:T(4,128)} %get-tuple-element.83) | copy-start | bytes 36868

commit v2 on v1

--- a/solution.py
+++ b/solution.py
@@ -12,7 +12,7 @@
 LANES = 128
 CHUNK = 256
 ROWS = 32
-AHEAD = 2
+AHEAD = 3
 
 beta_first = 0.9
 beta_second = 0.999
@@ -69,9 +69,9 @@
     q1_hbm,
     p2_hbm,
     q2_hbm,
-    logits_hbm,
-    igrad_hbm,
-    rms_ref,
+    lg_out,
+    ig_out,
+    sums_out,
     g1_out,
     w1_out,
     l1_out,
@@ -109,6 +109,7 @@
     w2t,
     tab,
     stage,
+    mt,
     mk,
     hp,
     hid,
@@ -126,7 +127,9 @@
     gb,
     rcore,
     rxy,
-    rz,
+    rzg,
+    rzv,
+    zs,
     ga,
     g1f,
     g1ft,
@@ -184,6 +187,7 @@
 
     core_peer = (flip(d, 1), m)
     z_order = sorted(range(1, M), reverse=True)
+    bits = [1 << k for k in range(M.bit_length() - 1)]
     xy_order = sorted(range(1, Q), reverse=True)
 
     def remote(src, dst, send, recv, peer):
@@ -246,7 +250,7 @@
             pltpu.make_async_copy(hbm.at[:, pl.ds(0, w)], block, own).wait()
 
     def send_out(kind, i):
-        buf, hbm = ((lgb, logits_hbm), (igb, igrad_hbm))[kind]
+        buf, hbm = ((lgb, lg_out), (igb, ig_out))[kind]
         col = multiple(i * w, w)
         there = pl.ds(multiple(m * mine + i * w, w), w)
         for o in z_order:
@@ -263,7 +267,7 @@
         ).start()
 
     def wait_out(kind, i):
-        buf, hbm = ((lgb, logits_hbm), (igb, igrad_hbm))[kind]
+        buf, hbm = ((lgb, lg_out), (igb, ig_out))[kind]
         part = buf.at[pl.ds(0, others), pl.ds(0, w)]
         remote(part, part, out_send.at[kind, i], out_recv.at[kind], z_peer(1)).wait_send()
         pltpu.make_async_copy(buf.at[pl.ds(0, F), pl.ds(0, w)], hbm.at[:, pl.ds(0, w)], out_own.at[kind, i]).wait()
@@ -271,23 +275,29 @@
     for load in loads[:4]:
         load.wait()
     wb[c, q, m, 0:dr, :] = w1_v[...].astype(BF16)
-    wb[c, q, m, dr : 2 * dr, :] = w2_v[...].T.astype(BF16)
+    wb[c, q, m, dr : 2 * dr, :] = w2_v[...].astype(BF16)
     for t in range(6):
         tb[c, q, m, t * kb : (t + 1) * kb, :] = mem_v[t]
 
+    def spread_z(bit, bufs, send, recv):
+        for h in range(0, M, 2 * bit):
+            slot, back = flip(m, h), flip(m, h + bit)
+            for k, buf in enumerate(bufs):
+                one, two = buf.at[c, q, slot], buf.at[c, q, back]
+                sems = (send.at[k, h + bit], recv.at[k, h + bit], z_peer(bit))
+                yield remote(one, one, *sems), remote(one, two, *sems)
+
     bufs = (wb, tb)
-    for o in z_order:
-        for k, buf in enumerate(bufs):
-            remote(buf.at[c, q, m], buf.at[c, q, m], wz_send.at[k, o], wz_recv.at[k, o], z_peer(o)).start()
-    for i in range(min(AHEAD, C)):
-        send_in(i)
+    first = list(spread_z(bits[-1], bufs, wz_send, wz_recv))
+    for go, _ in first:
+        go.start()
+    send_in(0)
 
     per_mask = LANES // K
     groups = mine // LANES
     start = multiple(m * groups * per_mask, groups * per_mask)
-    mk[...] = jnp.concatenate(
-        [mask_v[pl.ds(start + j, groups, stride=per_mask), :] for j in range(per_mask)], axis=1
-    ).astype(F32)
+    mt[...] = mask_v[...].astype(F32).T
+    mk[...] = jnp.concatenate([mt[pl.ds(start + j, groups, stride=per_mask), :] for j in range(per_mask)], axis=1)
 
     def clear(i, carry):
         rows = pl.ds(multiple(i * ROWS, ROWS), ROWS)
@@ -301,9 +311,16 @@
     stat[...] = jnp.zeros_like(stat)
 
     with jax.named_scope("weights_z"):
-        for o in z_order:
-            for k, buf in enumerate(bufs):
-                remote(buf.at[c, q, m], buf.at[c, q, flip(m, o)], wz_send.at[k, o], wz_recv.at[k, o], z_peer(o)).wait()
+        for bit in bits[::-1]:
+            if bit != bits[-1]:
+                first = list(spread_z(bit, bufs, wz_send, wz_recv))
+                for go, _ in first:
+                    go.start()
+            if bit == bits[0]:
+                for i in range(1, min(AHEAD, C)):
+                    send_in(i)
+            for _, come in first:
+                come.wait()
     with jax.named_scope("weights_xy"):
         for o in xy_order:
             for k, buf in enumerate(bufs):
@@ -576,22 +593,37 @@
 
             lax.fori_loop(0, M, step, 0)
     with jax.named_scope("sum_z"):
-        for o in z_order:
-            remote(gb.at[c, q, flip(m, o)], rz.at[o], gz_send.at[o], gz_recv.at[o], z_peer(o)).start()
-        pump(2)
-        for o in z_order:
-            remote(gb.at[c, q, flip(m, o)], rz.at[o], gz_send.at[o], gz_recv.at[o], z_peer(o)).wait()
-            gb[c, q, m] += rz[o]
+        slot = 0
+        for bit in bits:
+            moves = []
+            for h in range(0, M, 2 * bit):
+                away = flip(m, h + bit)
+                zs[slot] = gb[c, q, away, 0 : 2 * dr, :].astype(BF16)
+                sems = [(gz_send.at[k, slot], gz_recv.at[k, slot], z_peer(bit)) for k in range(2)]
+                tail = gb.at[c, q, away, pl.ds(2 * dr, pr - 2 * dr), :]
+                moves.append((slot, h, remote(zs.at[slot], rzg.at[slot], *sems[0]), remote(tail, rzv.at[slot], *sems[1])))
+                slot += 1
+            for _, _, one, two in moves:
+                one.start()
+                two.start()
+            pump()
+            for k, h, one, two in moves:
+                keep = flip(m, h)
+                one.wait()
+                two.wait()
+                gb[c, q, keep, 0 : 2 * dr, :] += rzg[k].astype(F32)
+                gb[c, q, keep, 2 * dr : pr, :] += rzv[k]
 
     total = gb[c, q, m]
     ga[c, q, m] = total[0 : 2 * dr, :].astype(BF16)
     with jax.named_scope("spread_z"):
-        for o in z_order:
-            remote(ga.at[c, q, m], ga.at[c, q, m], az_send.at[o], az_recv.at[o], z_peer(o)).start()
+        first = list(spread_z(bits[-1], (ga,), az_send, az_recv))
+        for go, _ in first:
+            go.start()
         for load in loads[4:]:
             load.wait()
         g1_out[...] = total[0:dr, :]
-        g2_out[...] = total[dr : 2 * dr, :].T
+        g2_out[...] = total[dr : 2 * dr, :]
         corr_one = 1.0 - beta_first**STEP
         corr_two = 1.0 - beta_second**STEP
         for t in range(6):
@@ -602,13 +634,15 @@
             m1_out[t] = one
             m2_out[t] = two
             mem_out[t] = mem_v[t] - adam_rate * (one / corr_one) / (jnp.sqrt(two / corr_two) + adam_eps)
-        row = 2 * dr + tr
-        count = total[row + 2 : row + 3, 0:1] * D
-        rms_ref[:, 0:1] = jnp.sqrt(total[row : row + 1, 0:1] / count)
-        rms_ref[:, 1:2] = jnp.sqrt(total[row + 1 : row + 2, 0:1] / count)
-        pump(2)
-        for o in z_order:
-            remote(ga.at[c, q, m], ga.at[c, q, flip(m, o)], az_send.at[o], az_recv.at[o], z_peer(o)).wait()
+        sums_out[...] = total[2 * dr + tr : pr, 0:LANES if F >= LANES else F]
+        for bit in bits[::-1]:
+            if bit != bits[-1]:
+                first = list(spread_z(bit, (ga,), az_send, az_recv))
+                for go, _ in first:
+                    go.start()
+            pump()
+            for _, come in first:
+                come.wait()
     with jax.named_scope("spread_xy"):
         for o in xy_order:
             remote(ga.at[c, q], ga.at[c, q], ax_send.at[o], ax_recv.at[o], xy_peer(o)).start()
@@ -649,23 +683,23 @@
 
         l1_out[...] = renewed(l1_v[...], mm_t(g1f[by_d, :], g1f[by_m, :]))
         r1_out[...] = renewed(r1_v[...], mm_t(g1ft[by_d, :], g1ft[by_m, :]))
-        l2_out[...] = renewed(l2_v[...], mm_t(g2f[by_m, :], g2f[by_d, :]))
-        r2_out[...] = renewed(r2_v[...], mm_t(g2ft[by_m, :], g2ft[by_d, :]))
-
-        def stepped(weight, left, grad_t, right):
-            first = mm_t(left[...], grad_t[...].astype(F32), high)
-            return weight[...] - shampoo_rate * mm_t(first, right[...], high)
-
-        w1_out[...] = stepped(w1_v, p1_v, g1ft, q1_v)
+        l2_out[...] = renewed(l2_v[...], mm_t(g2f[by_d, :], g2f[by_m, :]))
+        r2_out[...] = renewed(r2_v[...], mm_t(g2ft[by_d, :], g2ft[by_m, :]))
+
+        def stepped(weight, left, grad, right):
+            inner = jnp.dot(left[...], grad[...].astype(F32), precision=high, preferred_element_type=F32)
+            return weight[...] - shampoo_rate * mm_t(inner, right[...], high)
+
+        w1_out[...] = stepped(w1_v, p1_v, g1f, q1_v)
         pump(1)
-        w2_out[...] = stepped(w2_v, p2_v, g2ft, q2_v)
+        w2_out[...] = stepped(w2_v, q2_v, g2ft, p2_v)
 
     with jax.named_scope("drain"):
         pump(len(items))
         while state["done"] < len(items):
             wait_out(*items[state["done"]])
             state["done"] += 1
-        for kind, (buf, hbm) in enumerate(((lgb, logits_hbm), (igb, igrad_hbm))):
+        for kind, (buf, hbm) in enumerate(((lgb, lg_out), (igb, ig_out))):
             part = hbm.at[:, pl.ds(0, (M - 1) * mine)]
             remote(part, part, in_send, out_recv.at[kind], z_peer(1)).wait_recv()
         for buf in (xb, cb):
@@ -673,12 +707,27 @@
             remote(part, part, in_send, out_recv.at[0], z_peer(1)).wait_send()
 
 
+def finish(n_out, D, sums_ref, *refs):
+    outs, rms_ref, sems = refs[n_out : 2 * n_out], refs[2 * n_out], refs[2 * n_out + 1]
+    copies = [pltpu.make_async_copy(refs[i], outs[i], sems.at[i]) for i in range(n_out)]
+    for copy in copies:
+        copy.start()
+    sums = sums_ref[...]
+    ratio = jnp.sqrt(sums / (sums[2:3, :] * D))
+    rms_ref[0] = ratio[0, 0]
+    rms_ref[1] = ratio[1, 0]
+    for copy in copies:
+        copy.wait()
+
+
 def solution(mesh):
     N, M = mesh.shape["dp"], mesh.shape["mp"]
     Q = N // 2
 
     def on_device(*args):
         x, cot, mask, members, m1, m2, w1, w2, l1, r1, l2, r2, p1, q1, p2, q2 = args
+        mask, w2, l2, r2 = mask.T, w2.T, l2.T, r2.T
+        args = (x, cot, mask, members, m1, m2, w1, w2, l1, r1, l2, r2, p1, q1, p2, q2)
         F, R = x.shape
         D = F * M
         mine = R // M
@@ -691,38 +740,50 @@
         S = jax.ShapeDtypeStruct
         V = pltpu.VMEM
         dma = pltpu.SemaphoreType.DMA
-        outs = [S(x.shape, BF16), S(x.shape, BF16), S((1, 2), F32)]
+        outs = [S(x.shape, BF16), S(x.shape, BF16), S((8, min(F, LANES)), F32)]
         outs += [S(a.shape, F32) for a in (w1, w1, l1, r1, w2, w2, l2, r2, m1, m2, members)]
         scratch = [V(a.shape, a.dtype) for a in (mask, members, m1, m2, w1, w2, l1, r1, l2, r2, p1, q1, p2, q2)]
         scratch += [V((D, mine), BF16)] * 4
         scratch += [V((2, Q, M, 2 * dr, F), BF16), V((2, Q, M, tr, F), F32)]
         scratch += [V((D, D), BF16)] * 4
-        scratch += [V((6, D, LANES), F32), V((6, K, D), F32), V((mine // LANES, LANES), F32)]
+        scratch += [V((6, D, LANES), F32), V((6, K, D), F32), V(mask.shape[::-1], F32), V((mine // LANES, LANES), F32)]
         scratch += [V((D, w), F32)] * 4
         scratch += [V((D, w), BF16)] * 4
         scratch += [V((D, D), F32)] * 2
         scratch += [V((6, D, LANES), F32), V((6, K, D), F32), V((16, LANES), F32)]
-        scratch += [V((2, Q, M, pr, F), F32), V((Q, M, pr, F), F32), V((Q, M, pr, F), F32), V((M, pr, F), F32)]
+        scratch += [V((2, Q, M, pr, F), F32), V((Q, M, pr, F), F32), V((Q, M, pr, F), F32)]
+        scratch += [V((M - 1, 2 * dr, F), BF16), V((M - 1, pr - 2 * dr, F), F32), V((M - 1, 2 * dr, F), BF16)]
         scratch += [V((2, Q, M, 2 * dr, F), BF16)]
         scratch += [V((D, D), BF16)] * 4
         scratch += [dma((14,)), dma, dma((C,)), dma((C,)), dma((2, C)), dma((2, C)), dma((2, C)), dma((2,))]
         scratch += [dma((2, M)), dma((2, M)), dma((2, Q)), dma((2, Q)), dma((2,)), dma((2,))]
-        scratch += [dma((Q,)), dma((Q,)), dma((Q,)), dma((Q,)), dma((M,)), dma((M,))]
-        scratch += [dma((M,)), dma((M,)), dma((Q,)), dma((Q,)), dma, dma]
+        scratch += [dma((Q,)), dma((Q,)), dma((Q,)), dma((Q,)), dma((2, M)), dma((2, M))]
+        scratch += [dma((1, M)), dma((1, M)), dma((Q,)), dma((Q,)), dma, dma]
         hbm = pl.BlockSpec(memory_space=pl.ANY)
         vmem = pl.BlockSpec(memory_space=pltpu.VMEM)
         res = pl.pallas_call(
             functools.partial(kernel, N, M),
-            out_shape=outs,
-            in_specs=[hbm] * 16,
-            out_specs=[hbm] * 2 + [vmem] * 12,
+            out_shape=[V(a.shape, a.dtype) for a in outs],
+            in_specs=[pl.BlockSpec(memory_space=pl.ANY)] * 16,
+            out_specs=[pl.BlockSpec(memory_space=pl.ANY)] * 2 + [vmem] * 12,
             scratch_shapes=scratch,
             compiler_params=pltpu.CompilerParams(
-                collective_id=0, has_side_effects=True, vmem_limit_bytes=56 << 20
+                collective_id=0, has_side_effects=True, vmem_limit_bytes=42 << 20
             ),
             name="block",
-        )(*args)
-        return (res[0], res[1], res[2].reshape(2), *res[3:])
+        )(*[pltpu.with_memory_space_constraint(a, pltpu.HBM) for a in args])
+        kept = [*res[:2], *res[3:]]
+        done = pl.pallas_call(
+            functools.partial(finish, len(kept), D),
+            out_shape=[S(a.shape, a.dtype) for a in kept] + [S((2,), F32)],
+            in_specs=[vmem] + [pl.BlockSpec(memory_space=pl.ANY)] * len(kept),
+            out_specs=[hbm] * len(kept) + [pl.BlockSpec(memory_space=pltpu.SMEM)],
+            scratch_shapes=[dma((len(kept),))],
+            compiler_params=pltpu.CompilerParams(vmem_limit_bytes=16 << 20),
+            name="finish",
+        )(res[2], *kept)
+        logits, igrad, g1, n1, l1, r1, g2, n2, l2, r2, m1, m2, new, rms = done
+        return (logits, igrad, rms, g1, n1, l1, r1, g2.T, n2.T, l2.T, r2.T, m1, m2, new)
 
     placed = (
         P("mp", "dp"),

time: 226 us -> 198 us (0.88)
  local copies, waits for them, and re-layouts: 21.5 us -> 0 us
  Pallas kernels: 203 us -> 197 us
    unnamed x36 -> x0, local copies, waits for them, and re-layouts: 21.5 us -> none
    pallas_call x1 -> x2, Pallas kernels: 203 us -> 197 us  [the longest x1 194 us: on_device(): pl.pallas_call(functools.partial(kernel, N, M), out_shape=[V(a.shape, a.d...]
where the time goes in v2:
time: 198 us
  Pallas kernels  197 us (99%)
    pallas_call x1, Pallas kernels, on_device(): pl.pallas_call(functools.partial(kernel, N, M), out_shape=[V(a.shape, a.d...  194 us

profile of v2, /device:TPU:0, one launch (start us, length us, event | category | flops | bytes accessed | tf_op | source)
XLA Modules:
  0.0 197.7 jit_solution(3221083524935168294)
XLA Ops:
  0.7 194.3 %block.1 = (bf16[128,8192]{1,0:T(8,128)(2,1)S(1)}, bf16[128,8192]{1,0:T(8,128)(2,1)S(1)}, f32[8,128]{1,0:T(8,128)S(1)}, f32[64,128]{1,0:T(8,128)S(1)}, f32[64,12...) custom-call(bf16[128,8192]{1,0:T(8,128)(2,1)} %x_hbm.1, ...), custom_call_target="tpu_custom_call" | custom-call | tf_op jit(solution)/shard_map/block/pallas_call | solution.py:764
  195.0 2.7 %finish.1 = (bf16[128,8192]{1,0:T(8,128)(2,1)}, bf16[128,8192]{1,0:T(8,128)(2,1)}, f32[64,128]{1,0:T(8,128)}, f32[64,128]{1,0:T(8,128)}, f32[64,128]{1,0:T(8,128...) custom-call(f32[8,128]{1,0:T(8,128)S(1)} %get-tuple-element.42.sums_, ...), custom_call_target="tpu_custom_call" | custom-call | tf_op jit(solution)/shard_map/finish/pallas_call | solution.py:776

commit v3 on v2

--- a/solution.py
+++ b/solution.py
@@ -12,7 +12,10 @@
 LANES = 128
 CHUNK = 256
 ROWS = 32
-AHEAD = 3
+AHEAD = 2
+FIRST = 4
+OUT = 4
+LEAST = 8
 
 beta_first = 0.9
 beta_second = 0.999
@@ -53,6 +56,7 @@
 def kernel(
     N,
     M,
+    cap,
     x_hbm,
     cot_hbm,
     mask_hbm,
@@ -97,6 +101,10 @@
     q1_v,
     p2_v,
     q2_v,
+    cv,
+    cp,
+    st,
+    igr,
     xb,
     cb,
     lgb,
@@ -111,6 +119,7 @@
     stage,
     mt,
     mk,
+    rk,
     hp,
     hid,
     dgm,
@@ -119,6 +128,8 @@
     hi,
     gp,
     gpre,
+    cx,
+    ig,
     g1,
     g2t,
     vec,
@@ -126,7 +137,9 @@
     stat,
     gb,
     rcore,
-    rxy,
+    xs,
+    rxg,
+    rxv,
     rzg,
     rzv,
     zs,
@@ -169,6 +182,9 @@
     w = min(CHUNK, mine)
     C = mine // w
     tiles = w // LANES
+    packed = cap < mine
+    KC = cap // w
+    groups = mine // LANES
     kb = K // N
     dr = D // N
     tr = tb.shape[3]
@@ -211,6 +227,8 @@
         (p2_hbm, p2_v),
         (q2_hbm, q2_v),
     )
+    if packed:
+        pairs = (*pairs, (cot_hbm, cv))
     loads = [pltpu.make_async_copy(a, b, local_sem.at[i]) for i, (a, b) in enumerate(pairs)]
     for load in loads:
         load.start()
@@ -222,55 +240,116 @@
             pl.semaphore_signal(entry, inc=1, device_id=peer, device_id_type=MESH)
         pl.semaphore_wait(entry, len(peers))
 
-    def send_in(i):
-        col = multiple(i * w, w)
+    kinds_in = ((xb, x_recv, 0), (cb, c_recv, 1))
+
+    def send_in(i, kinds=(0, 1)):
         here = pl.ds(multiple(m * F, F), F)
-        for hbm, buf, sem in ((x_hbm, xb, x_recv), (cot_hbm, cb, c_recv)):
+        col = pl.ds(multiple(i * w, w), w)
+
+        def source(kind, to):
+            if kind and packed:
+                return cp.at[to, :, col]
+            return (x_hbm, cot_hbm)[kind].at[:, pl.ds(multiple(to * mine + i * w, w), w)]
+
+        def start(kind):
+            buf, sem, _ = kinds_in[kind]
             for o in z_order:
                 to = flip(m, o)
-                remote(
-                    hbm.at[:, pl.ds(multiple(to * mine + i * w, w), w)],
-                    buf.at[here, pl.ds(col, w)],
-                    in_send,
-                    sem.at[i],
-                    (d, to),
-                ).start()
-        for hbm, buf, sem in ((x_hbm, xb, own_sem.at[0, i]), (cot_hbm, cb, own_sem.at[1, i])):
-            pltpu.make_async_copy(
-                hbm.at[:, pl.ds(multiple(m * mine + i * w, w), w)], buf.at[here, pl.ds(col, w)], sem
-            ).start()
+                remote(source(kind, to), buf.at[here, col], in_send.at[kind], sem.at[i], (d, to)).start()
+            pltpu.make_async_copy(source(kind, m), buf.at[here, col], own_sem.at[kind, i]).start()
+
+        for kind in kinds:
+            if kind and packed and not isinstance(i, int):
+                pl.when(i < KC)(lambda: start(1))
+            elif not (kind and packed) or i < KC:
+                start(kind)
 
     others = (M - 1) * F
 
     def wait_in(i):
-        for hbm, buf, sem, own in ((x_hbm, xb, x_recv, own_sem.at[0, i]), (cot_hbm, cb, c_recv, own_sem.at[1, i])):
+        def arrive(kind):
+            buf, sem, _ = kinds_in[kind]
             part = buf.at[pl.ds(0, others), pl.ds(0, w)]
-            remote(part, part, in_send, sem.at[i], z_peer(1)).wait_recv()
+            remote(part, part, in_send.at[kind], sem.at[i], z_peer(1)).wait_recv()
             block = buf.at[pl.ds(0, F), pl.ds(0, w)]
-            pltpu.make_async_copy(hbm.at[:, pl.ds(0, w)], block, own).wait()
+            pltpu.make_async_copy(block, block, own_sem.at[kind, i]).wait()
+
+        arrive(0)
+        if packed:
+            pl.when(i < KC)(lambda: arrive(1))
+        else:
+            arrive(1)
 
     def send_out(kind, i):
-        buf, hbm = ((lgb, lg_out), (igb, ig_out))[kind]
-        col = multiple(i * w, w)
-        there = pl.ds(multiple(m * mine + i * w, w), w)
+        col = pl.ds(multiple(i * w, w), w)
+        if kind and packed:
+            there = igr.at[m, :, col]
+        else:
+            there = (lg_out, ig_out)[kind].at[:, pl.ds(multiple(m * mine + i * w, w), w)]
+        buf = (lgb, igb)[kind]
         for o in z_order:
             to = flip(m, o)
+            recv = out_recv.at[kind, o] if kind and packed else out_recv.at[kind, 0]
             remote(
-                buf.at[pl.ds(multiple(to * F, F), F), pl.ds(col, w)],
-                hbm.at[:, there],
-                out_send.at[kind, i],
-                out_recv.at[kind],
-                (d, to),
+                buf.at[pl.ds(multiple(to * F, F), F), col], there, out_send.at[kind, i], recv, (d, to)
             ).start()
-        pltpu.make_async_copy(
-            buf.at[pl.ds(multiple(m * F, F), F), pl.ds(col, w)], hbm.at[:, there], out_own.at[kind, i]
-        ).start()
+        if not (kind and packed):
+            pltpu.make_async_copy(buf.at[pl.ds(multiple(m * F, F), F), col], there, out_own.at[kind, i]).start()
 
     def wait_out(kind, i):
-        buf, hbm = ((lgb, lg_out), (igb, ig_out))[kind]
+        buf = (lgb, igb)[kind]
         part = buf.at[pl.ds(0, others), pl.ds(0, w)]
-        remote(part, part, out_send.at[kind, i], out_recv.at[kind], z_peer(1)).wait_send()
-        pltpu.make_async_copy(buf.at[pl.ds(0, F), pl.ds(0, w)], hbm.at[:, pl.ds(0, w)], out_own.at[kind, i]).wait()
+        remote(part, part, out_send.at[kind, i], out_recv.at[kind, 0], z_peer(1)).wait_send()
+        if not (kind and packed):
+            own = buf.at[pl.ds(0, F), pl.ds(0, w)]
+            pltpu.make_async_copy(own, own, out_own.at[kind, i]).wait()
+
+    line = lax.broadcasted_iota(jnp.int32, (w, LANES), 0).astype(F32)
+
+    def matches(p, k, i):
+        base = (k * w) * jnp.float32(1) if isinstance(k, int) else (k * w).astype(F32)
+        parts = []
+        for j in range(tiles):
+            row = rk[pl.ds(p * groups + i * tiles + j, 1), :] - base
+            parts.append(jnp.where(line == row, 1.0, 0.0).astype(BF16))
+        return jnp.concatenate(parts, axis=1)
+
+    spread_by = K // LEAST
+
+    def pack_block(k, p):
+        def step(i, acc):
+            cols = pl.ds(multiple(p * mine + i * w, w), w)
+            return acc + mm_t(cv[:, cols], matches(p, k, i))
+
+        acc = lax.fori_loop(k, min(C, spread_by * k + spread_by), step, jnp.zeros((F, w), F32))
+        cp[p, :, k * w : (k + 1) * w] = acc.astype(BF16)
+
+    def pack_chunk(k):
+        with jax.named_scope("pack_cot"):
+
+            def step(p, carry):
+                pack_block(k, p)
+                return carry
+
+            lax.fori_loop(0, M, step, 0)
+
+    def unpack_block(p):
+        with jax.named_scope("unpack"):
+
+            def chunk(i, carry):
+                def step(k, acc):
+                    return acc + mm(igr[p, :, pl.ds(multiple(k * w, w), w)], matches(p, k, i))
+
+                acc = lax.fori_loop(i // spread_by, jnp.minimum(i, KC - 1) + 1, step, jnp.zeros((F, w), F32))
+                ig_out[:, pl.ds(multiple(p * mine + i * w, w), w)] = acc.astype(BF16)
+                return carry
+
+            lax.fori_loop(0, C, chunk, 0)
+
+    def unpack_from(o):
+        part = igr.at[0]
+        remote(part, part, in_send.at[0], out_recv.at[1, o], z_peer(o)).wait_recv()
+        unpack_block(flip(m, o))
 
     for load in loads[:4]:
         load.wait()
@@ -291,13 +370,23 @@
     first = list(spread_z(bits[-1], bufs, wz_send, wz_recv))
     for go, _ in first:
         go.start()
-    send_in(0)
-
     per_mask = LANES // K
-    groups = mine // LANES
-    start = multiple(m * groups * per_mask, groups * per_mask)
     mt[...] = mask_v[...].astype(F32).T
-    mk[...] = jnp.concatenate([mt[pl.ds(start + j, groups, stride=per_mask), :] for j in range(per_mask)], axis=1)
+    mk[...] = jnp.concatenate(
+        [mt[pl.ds(j, M * groups, stride=per_mask), :] for j in range(per_mask)], axis=1
+    )
+    if packed:
+        flags = mk[...]
+        rows, cols = M * groups, LANES
+        lower = lax.broadcasted_iota(jnp.int32, (cols, cols), 0) < lax.broadcasted_iota(jnp.int32, (cols, cols), 1)
+        inside = mm(flags.astype(BF16), jnp.where(lower, 1.0, 0.0).astype(BF16))
+        sums = jnp.broadcast_to(jnp.sum(flags, axis=1, keepdims=True), (rows, cols)).astype(BF16)
+        one = lax.broadcasted_iota(jnp.int32, (rows, rows), 0)
+        two = lax.broadcasted_iota(jnp.int32, (rows, rows), 1)
+        ahead = (two < one) & (two >= one - one % groups)
+        place_in = inside + mm(jnp.where(ahead, 1.0, 0.0).astype(BF16), sums)
+        rk[...] = jnp.where(flags > 0.0, place_in, -1.0)
+    send_in(0, (0,) if packed else (0, 1))
 
     def clear(i, carry):
         rows = pl.ds(multiple(i * ROWS, ROWS), ROWS)
@@ -309,6 +398,29 @@
 
     lax.fori_loop(0, blocks, clear, 0)
     stat[...] = jnp.zeros_like(stat)
+    if packed:
+
+        def clear_packed(i, carry):
+            igb[pl.ds(multiple(i * ROWS, ROWS), ROWS), :] = jnp.zeros((ROWS, cap), BF16)
+            return carry
+
+        lax.fori_loop(0, blocks, clear_packed, 0)
+
+    ahead_of = min(FIRST, C)
+    if packed:
+        loads[-1].wait()
+        pack_chunk(0)
+
+    def step_in(k):
+        if packed:
+            if k < KC:
+                send_in(k, (1,))
+            if k + 1 < ahead_of:
+                send_in(k + 1, (0,))
+            if k + 1 < KC:
+                pack_chunk(k + 1)
+        elif k + 1 < ahead_of:
+            send_in(k + 1)
 
     with jax.named_scope("weights_z"):
         for bit in bits[::-1]:
@@ -317,20 +429,26 @@
                 for go, _ in first:
                     go.start()
             if bit == bits[0]:
-                for i in range(1, min(AHEAD, C)):
-                    send_in(i)
+                step_in(0)
             for _, come in first:
                 come.wait()
     with jax.named_scope("weights_xy"):
         for o in xy_order:
             for k, buf in enumerate(bufs):
                 remote(buf.at[c, q], buf.at[c, q], wx_send.at[k, o], wx_recv.at[k, o], xy_peer(o)).start()
+        step_in(1)
+        step_in(2)
         for o in xy_order:
             for k, buf in enumerate(bufs):
                 remote(buf.at[c, q], buf.at[c, flip(q, o)], wx_send.at[k, o], wx_recv.at[k, o], xy_peer(o)).wait()
     with jax.named_scope("weights_core"):
         for k, buf in enumerate(bufs):
             remote(buf.at[c], buf.at[c], wc_send.at[k], wc_recv.at[k], core_peer).start()
+        for k in range(3, max(ahead_of, KC if packed else 0)):
+            if k < ahead_of:
+                step_in(k)
+            elif k + 1 < KC:
+                pack_chunk(k + 1)
         for k, buf in enumerate(bufs):
             remote(buf.at[c], buf.at[1 - c], wc_send.at[k], wc_recv.at[k], core_peer).wait()
 
@@ -374,23 +492,25 @@
     def eight(value):
         return value.reshape(ROWS // 8, 8, LANES).sum(0)
 
+    if packed:
+        early = [(C - 3, [(0, 0)]), (C - 2, [(0, 1)]), (C - 1, [(0, 2)])]
+    else:
+        early = [(C - 2, [(0, 0), (1, 0)]), (C - 1, [(0, 1), (1, 1)])]
+
     def work(i, carry):
         col = multiple(i * w, w)
         with jax.named_scope("wait_in"):
             wait_in(i)
 
-        @pl.when(i + AHEAD < C)
+        @pl.when((i + AHEAD >= FIRST) & (i + AHEAD < C))
         def _():
             send_in(i + AHEAD)
 
-        first_out = max(C - 2, 0)
-
-        @pl.when(i >= first_out)
-        def _():
-            for kind in range(2):
-                send_out(kind, i - first_out)
-
-        masks = [mk[pl.ds(i * tiles + j, 1), :] for j in range(tiles)]
+        for late, parts in early:
+            for kind, k in parts:
+                pl.when(i == late)(functools.partial(send_out, kind, k))
+
+        masks = [mk[pl.ds(m * groups + i * tiles + j, 1), :] for j in range(tiles)]
 
         def place_of(r):
             return pl.ds(multiple(r * ROWS, ROWS), ROWS)
@@ -434,6 +554,23 @@
             lax.fori_loop(0, blocks, curve_rows, 0)
         with jax.named_scope("mm_two"):
             prod[...] = mm(w2t[...], hi[...])
+        low, high_k = i // spread_by, jnp.minimum(i, KC - 1)
+        if packed:
+            with jax.named_scope("expand"):
+
+                def grow(k, carry):
+                    st[k] = matches(m, k, i)
+                    cx[...] += mm(cb[:, pl.ds(multiple(k * w, w), w)], st[k])
+                    return carry
+
+                cx[...] = jnp.zeros_like(cx)
+                lax.fori_loop(low, high_k + 1, grow, 0)
+
+        def grad_of(rows, j):
+            if packed:
+                return cx[rows, j * LANES : (j + 1) * LANES]
+            return cb[rows, lanes_of(j)].astype(F32) * masks[j]
+
 
         def out_rows(r, sums):
             rows = place_of(r)
@@ -447,7 +584,7 @@
                 branch = projected * gain + bias
                 lgb[rows, lanes_of(j)] = (x + branch).astype(BF16)
                 new.append(sums[j] + eight(branch * branch))
-                go = cb[rows, lanes_of(j)].astype(F32) * masks[j]
+                go = grad_of(rows, j)
                 v5 = v5 + go
                 v4 = v4 + go * projected
                 gp[rows, cols] = (go * gain).astype(BF16)
@@ -501,29 +638,50 @@
                 cols = slice(j * LANES, (j + 1) * LANES)
                 gs = prod[rows, cols]
                 v0 = v0 + gs * xb[rows, lanes_of(j)].astype(F32)
-                go = cb[rows, lanes_of(j)].astype(F32) * masks[j]
-                igb[rows, lanes_of(j)] = (gs * row_in + go).astype(BF16)
+                go = grad_of(rows, j)
+                done = (gs * row_in + go).astype(BF16)
+                if packed:
+                    ig[rows, cols] = done
+                else:
+                    igb[rows, lanes_of(j)] = done
             vec[0, rows, :] = v0
             return carry
 
         with jax.named_scope("in"):
             lax.fori_loop(0, blocks, in_rows, 0)
+        if packed:
+            ig_out[:, pl.ds(multiple(m * mine + col, w), w)] = ig[pl.ds(multiple(m * F, F), F), :]
+            with jax.named_scope("shrink"):
+
+                def shrink(k, carry):
+                    cols = pl.ds(multiple(k * w, w), w)
+                    igb[:, cols] = (igb[:, cols].astype(F32) + mm_t(ig[...], st[k])).astype(BF16)
+                    return carry
+
+                lax.fori_loop(low, high_k + 1, shrink, 0)
         return carry
 
     lax.fori_loop(0, C, work, 0)
 
-    items = [(kind, i) for i in range(C) for kind in range(2)]
-    already = 2 * min(C, 2)
+    items = [item for _, parts in early for item in parts]
+    already = len(items)
+    if packed:
+        items += [(1, k) for k in range(KC)] + [(0, i) for i in range(3, C)]
+    else:
+        items += [(kind, i) for i in range(2, C) for kind in range(2)]
     state = {"sent": already, "done": 0}
 
-    def pump(count=1):
+    def pump(count, most=OUT):
         with jax.named_scope("pump"):
             for _ in range(count):
                 if state["sent"] < len(items):
-                    wait_out(*items[state["done"]])
-                    state["done"] += 1
+                    while state["sent"] - state["done"] >= most:
+                        wait_out(*items[state["done"]])
+                        state["done"] += 1
                     send_out(*items[state["sent"]])
                     state["sent"] += 1
+
+    pump(2)
 
     with jax.named_scope("pack"):
 
@@ -550,8 +708,10 @@
                 for j in range(M):
                     row = 2 * dr + t * kb
                     gb[i % 2, i // 2, j, row : row + kb, :] = vt[t, i * kb : (i + 1) * kb, j * F : (j + 1) * F]
-        totals = [stat[0:8, :], stat[8:16, :], jnp.pad(mk[...], ((0, -groups % 8), (0, 0)))]
+        own = mk[pl.ds(multiple(m * groups, groups), groups), :]
+        totals = [stat[0:8, :], stat[8:16, :], own]
         rows8 = [jnp.sum(v, keepdims=True).reshape(1, 1) for v in totals]
+        rows8.append(jnp.where(rows8[2] > cap, 1.0, 0.0))
         row_id = lax.broadcasted_iota(jnp.int32, (8, F), 0)
         lines = sum(jnp.where(row_id == k, v, 0.0) for k, v in enumerate(rows8))
 
@@ -562,7 +722,6 @@
 
         lax.fori_loop(0, N, put, 0)
 
-    pump()
     with jax.named_scope("sum_core"):
         for o in xy_order + [0]:
             k = flip(q, o)
@@ -574,21 +733,34 @@
                 return carry
 
             lax.fori_loop(0, M, step, 0)
+
+        def over_xy(o):
+            k = flip(q, o)
+            sems = [(gx_send.at[n, o], gx_recv.at[n, o], xy_peer(o)) for n in range(2)]
+            tail = gb.at[c, k, :, pl.ds(2 * dr, pr - 2 * dr), :]
+            return remote(xs.at[o], rxg.at[o], *sems[0]), remote(tail, rxv.at[o], *sems[1])
 
         for o in xy_order + [0]:
             k = flip(q, o)
             remote(gb.at[1 - c, k], rcore.at[k], gc_send.at[o], gc_recv.at[o], core_peer).wait()
             add_core(k)
             if o:
-                remote(gb.at[c, k], rxy.at[o], gx_send.at[o], gx_recv.at[o], xy_peer(o)).start()
-    pump(2)
+
+                def round_piece(j, carry):
+                    xs[o, j] = gb[c, k, j, 0 : 2 * dr, :].astype(BF16)
+                    return carry
+
+                lax.fori_loop(0, M, round_piece, 0)
+                for copy in over_xy(o):
+                    copy.start()
     with jax.named_scope("sum_xy"):
         for o in xy_order:
-            k = flip(q, o)
-            remote(gb.at[c, k], rxy.at[o], gx_send.at[o], gx_recv.at[o], xy_peer(o)).wait()
+            for copy in over_xy(o):
+                copy.wait()
 
             def step(j, carry):
-                gb[c, q, j] += rxy[o, j]
+                gb[c, q, j, 0 : 2 * dr, :] += rxg[o, j].astype(F32)
+                gb[c, q, j, 2 * dr : pr, :] += rxv[o, j]
                 return carry
 
             lax.fori_loop(0, M, step, 0)
@@ -606,7 +778,7 @@
             for _, _, one, two in moves:
                 one.start()
                 two.start()
-            pump()
+            pump(3 if bit == bits[0] else 2)
             for k, h, one, two in moves:
                 keep = flip(m, h)
                 one.wait()
@@ -617,10 +789,13 @@
     total = gb[c, q, m]
     ga[c, q, m] = total[0 : 2 * dr, :].astype(BF16)
     with jax.named_scope("spread_z"):
-        first = list(spread_z(bits[-1], (ga,), az_send, az_recv))
-        for go, _ in first:
-            go.start()
-        for load in loads[4:]:
+
+        def over_z(o, slot):
+            return remote(ga.at[c, q, m], ga.at[c, q, slot], az_send.at[o], az_recv.at[o], z_peer(o))
+
+        for o in z_order:
+            over_z(o, m).start()
+        for load in loads[4:14]:
             load.wait()
         g1_out[...] = total[0:dr, :]
         g2_out[...] = total[dr : 2 * dr, :]
@@ -635,25 +810,23 @@
             m2_out[t] = two
             mem_out[t] = mem_v[t] - adam_rate * (one / corr_one) / (jnp.sqrt(two / corr_two) + adam_eps)
         sums_out[...] = total[2 * dr + tr : pr, 0:LANES if F >= LANES else F]
-        for bit in bits[::-1]:
-            if bit != bits[-1]:
-                first = list(spread_z(bit, (ga,), az_send, az_recv))
-                for go, _ in first:
-                    go.start()
-            pump()
-            for _, come in first:
-                come.wait()
+        pump(len(items), len(items))
+        if packed:
+            for o in z_order[:-1]:
+                unpack_from(o)
+        for o in z_order:
+            over_z(o, flip(m, o)).wait()
     with jax.named_scope("spread_xy"):
         for o in xy_order:
             remote(ga.at[c, q], ga.at[c, q], ax_send.at[o], ax_recv.at[o], xy_peer(o)).start()
-        pump(1)
+        if packed:
+            for o in z_order[-1:]:
+                unpack_from(o)
         for o in xy_order:
             remote(ga.at[c, q], ga.at[c, flip(q, o)], ax_send.at[o], ax_recv.at[o], xy_peer(o)).wait()
     with jax.named_scope("spread_core"):
         remote(ga.at[c], ga.at[c], ac_send, ac_recv, core_peer).start()
         remote(ga.at[c], ga.at[1 - c], ac_send, ac_recv, core_peer).wait()
-    pump(1)
-
     with jax.named_scope("shampoo"):
 
         def place_g(i, carry):
@@ -691,24 +864,23 @@
             return weight[...] - shampoo_rate * mm_t(inner, right[...], high)
 
         w1_out[...] = stepped(w1_v, p1_v, g1f, q1_v)
-        pump(1)
         w2_out[...] = stepped(w2_v, q2_v, g2ft, p2_v)
 
     with jax.named_scope("drain"):
-        pump(len(items))
         while state["done"] < len(items):
             wait_out(*items[state["done"]])
             state["done"] += 1
-        for kind, (buf, hbm) in enumerate(((lgb, lg_out), (igb, ig_out))):
-            part = hbm.at[:, pl.ds(0, (M - 1) * mine)]
-            remote(part, part, in_send, out_recv.at[kind], z_peer(1)).wait_recv()
-        for buf in (xb, cb):
-            part = buf.at[pl.ds(0, others), pl.ds(0, mine)]
-            remote(part, part, in_send, out_recv.at[0], z_peer(1)).wait_send()
+        for kind, out in enumerate((lg_out,) if packed else (lg_out, ig_out)):
+            part = out.at[:, pl.ds(0, (M - 1) * mine)]
+            remote(part, part, in_send.at[kind], out_recv.at[kind, 0], z_peer(1)).wait_recv()
+        for kind, buf in enumerate((xb, cb)):
+            part = buf.at[pl.ds(0, others), :]
+            remote(part, part, in_send.at[kind], out_recv.at[0, 0], z_peer(1)).wait_send()
 
 
 def finish(n_out, D, sums_ref, *refs):
-    outs, rms_ref, sems = refs[n_out : 2 * n_out], refs[2 * n_out], refs[2 * n_out + 1]
+    outs = refs[n_out : 2 * n_out]
+    rms_ref, flag_ref, sems = refs[2 * n_out :]
     copies = [pltpu.make_async_copy(refs[i], outs[i], sems.at[i]) for i in range(n_out)]
     for copy in copies:
         copy.start()
@@ -716,6 +888,7 @@
     ratio = jnp.sqrt(sums / (sums[2:3, :] * D))
     rms_ref[0] = ratio[0, 0]
     rms_ref[1] = ratio[1, 0]
+    flag_ref[0] = jnp.where(sums[3, 0] > 0.0, 1, 0)
     for copy in copies:
         copy.wait()
 
@@ -737,51 +910,69 @@
         dr = w1.shape[0]
         tr = -(-6 * kb // 8) * 8
         pr = 2 * dr + tr + 8
+        groups = mine // LANES
         S = jax.ShapeDtypeStruct
         V = pltpu.VMEM
         dma = pltpu.SemaphoreType.DMA
         outs = [S(x.shape, BF16), S(x.shape, BF16), S((8, min(F, LANES)), F32)]
         outs += [S(a.shape, F32) for a in (w1, w1, l1, r1, w2, w2, l2, r2, m1, m2, members)]
-        scratch = [V(a.shape, a.dtype) for a in (mask, members, m1, m2, w1, w2, l1, r1, l2, r2, p1, q1, p2, q2)]
-        scratch += [V((D, mine), BF16)] * 4
-        scratch += [V((2, Q, M, 2 * dr, F), BF16), V((2, Q, M, tr, F), F32)]
-        scratch += [V((D, D), BF16)] * 4
-        scratch += [V((6, D, LANES), F32), V((6, K, D), F32), V(mask.shape[::-1], F32), V((mine // LANES, LANES), F32)]
-        scratch += [V((D, w), F32)] * 4
-        scratch += [V((D, w), BF16)] * 4
-        scratch += [V((D, D), F32)] * 2
-        scratch += [V((6, D, LANES), F32), V((6, K, D), F32), V((16, LANES), F32)]
-        scratch += [V((2, Q, M, pr, F), F32), V((Q, M, pr, F), F32), V((Q, M, pr, F), F32)]
-        scratch += [V((M - 1, 2 * dr, F), BF16), V((M - 1, pr - 2 * dr, F), F32), V((M - 1, 2 * dr, F), BF16)]
-        scratch += [V((2, Q, M, 2 * dr, F), BF16)]
-        scratch += [V((D, D), BF16)] * 4
-        scratch += [dma((14,)), dma, dma((C,)), dma((C,)), dma((2, C)), dma((2, C)), dma((2, C)), dma((2,))]
-        scratch += [dma((2, M)), dma((2, M)), dma((2, Q)), dma((2, Q)), dma((2,)), dma((2,))]
-        scratch += [dma((Q,)), dma((Q,)), dma((Q,)), dma((Q,)), dma((2, M)), dma((2, M))]
-        scratch += [dma((1, M)), dma((1, M)), dma((Q,)), dma((Q,)), dma, dma]
-        hbm = pl.BlockSpec(memory_space=pl.ANY)
+        anywhere = pl.BlockSpec(memory_space=pl.ANY)
         vmem = pl.BlockSpec(memory_space=pltpu.VMEM)
-        res = pl.pallas_call(
-            functools.partial(kernel, N, M),
-            out_shape=[V(a.shape, a.dtype) for a in outs],
-            in_specs=[pl.BlockSpec(memory_space=pl.ANY)] * 16,
-            out_specs=[pl.BlockSpec(memory_space=pl.ANY)] * 2 + [vmem] * 12,
-            scratch_shapes=scratch,
-            compiler_params=pltpu.CompilerParams(
-                collective_id=0, has_side_effects=True, vmem_limit_bytes=42 << 20
-            ),
-            name="block",
-        )(*[pltpu.with_memory_space_constraint(a, pltpu.HBM) for a in args])
-        kept = [*res[:2], *res[3:]]
-        done = pl.pallas_call(
-            functools.partial(finish, len(kept), D),
-            out_shape=[S(a.shape, a.dtype) for a in kept] + [S((2,), F32)],
-            in_specs=[vmem] + [pl.BlockSpec(memory_space=pl.ANY)] * len(kept),
-            out_specs=[hbm] * len(kept) + [pl.BlockSpec(memory_space=pltpu.SMEM)],
-            scratch_shapes=[dma((len(kept),))],
-            compiler_params=pltpu.CompilerParams(vmem_limit_bytes=16 << 20),
-            name="finish",
-        )(res[2], *kept)
+        smem = pl.BlockSpec(memory_space=pltpu.SMEM)
+
+        def run(cap, number):
+            packed = cap < mine
+            KC = cap // w
+
+            def only(shape, dtype):
+                return V(shape if packed else (16, LANES), dtype)
+
+            scratch = [V(a.shape, a.dtype) for a in (mask, members, m1, m2, w1, w2, l1, r1, l2, r2, p1, q1, p2, q2)]
+            scratch += [only((F, R), BF16), only((M, F, cap), BF16), only((KC, w, w), BF16), only((M, F, cap), BF16)]
+            scratch += [V((D, mine), BF16), V((D, cap), BF16), V((D, mine), BF16), V((D, cap), BF16)]
+            scratch += [V((2, Q, M, 2 * dr, F), BF16), V((2, Q, M, tr, F), F32)]
+            scratch += [V((D, D), BF16)] * 4
+            scratch += [V((6, D, LANES), F32), V((6, K, D), F32), V(mask.shape[::-1], F32)]
+            scratch += [V((M * groups, LANES), F32), V((M * groups, LANES), F32)]
+            scratch += [V((D, w), F32)] * 4
+            scratch += [V((D, w), BF16)] * 4
+            scratch += [only((D, w), F32), only((D, w), BF16)]
+            scratch += [V((D, D), F32)] * 2
+            scratch += [V((6, D, LANES), F32), V((6, K, D), F32), V((16, LANES), F32)]
+            scratch += [V((2, Q, M, pr, F), F32), V((Q, M, pr, F), F32)]
+            scratch += [V((Q, M, 2 * dr, F), BF16), V((Q, M, 2 * dr, F), BF16), V((Q, M, pr - 2 * dr, F), F32)]
+            scratch += [V((M - 1, 2 * dr, F), BF16), V((M - 1, pr - 2 * dr, F), F32), V((M - 1, 2 * dr, F), BF16)]
+            scratch += [V((2, Q, M, 2 * dr, F), BF16)]
+            scratch += [V((D, D), BF16)] * 4
+            scratch += [dma((15,)), dma((2,)), dma((C,)), dma((C,)), dma((2, C)), dma((2, C)), dma((2, C)), dma((2, M))]
+            scratch += [dma((2, M)), dma((2, M)), dma((2, Q)), dma((2, Q)), dma((2,)), dma((2,))]
+            scratch += [dma((Q,)), dma((Q,)), dma((2, Q)), dma((2, Q)), dma((2, M)), dma((2, M))]
+            scratch += [dma((M,)), dma((M,)), dma((Q,)), dma((Q,)), dma, dma]
+            res = pl.pallas_call(
+                functools.partial(kernel, N, M, cap),
+                out_shape=[V(a.shape, a.dtype) for a in outs],
+                in_specs=[anywhere] * 16,
+                out_specs=[vmem] * 14,
+                scratch_shapes=scratch,
+                compiler_params=pltpu.CompilerParams(
+                    collective_id=number, has_side_effects=True, vmem_limit_bytes=46 << 20
+                ),
+                name="packed" if packed else "whole",
+            )(*[pltpu.with_memory_space_constraint(a, pltpu.HBM) for a in args])
+            kept = [*res[:2], *res[3:]]
+            *done, rms, flag = pl.pallas_call(
+                functools.partial(finish, len(kept), D),
+                out_shape=[S(a.shape, a.dtype) for a in kept] + [S((2,), F32), S((1,), jnp.int32)],
+                in_specs=[vmem] + [anywhere] * len(kept),
+                out_specs=[anywhere] * len(kept) + [smem] * 2,
+                scratch_shapes=[dma((len(kept),))],
+                compiler_params=pltpu.CompilerParams(vmem_limit_bytes=16 << 20),
+                name="finish",
+            )(res[2], *kept)
+            return flag, (*done, rms)
+
+        flag, fast = run(mine * 3 // 4, 0)
+        done = lax.cond(flag[0] > 0, lambda: run(mine, 1)[1], lambda: fast)
         logits, igrad, g1, n1, l1, r1, g2, n2, l2, r2, m1, m2, new, rms = done
         return (logits, igrad, rms, g1, n1, l1, r1, g2.T, n2.T, l2.T, r2.T, m1, m2, new)
 

time: 198 us -> 178 us (0.90)
  Pallas kernels: 197 us -> 176 us
    pallas_call x2, Pallas kernels: 197 us -> 176 us  [the longest x1 173 us: run(): pl.pallas_call(functools.partial(kernel, N, M, cap), out_shape=[V(a.shape...]
where the time goes in v3:
time: 178 us; the launch traced here: 177 us
  Pallas kernels  176 us (99%)
    pallas_call x1, Pallas kernels, run(): pl.pallas_call(functools.partial(kernel, N, M, cap), out_shape=[V(a.shape...  173 us

profile of v3, /device:TPU:0, one launch (start us, length us, event | category | flops | bytes accessed | tf_op | source)
XLA Modules:
  0.0 177.4 jit_solution(15933816900651496869)
XLA Ops:
  0.6 173.0 %packed.1 = (bf16[128,8192]{1,0:T(8,128)(2,1)S(1)}, bf16[128,8192]{1,0:T(8,128)(2,1)S(1)}, f32[8,128]{1,0:T(8,128)S(1)}, f32[64,128]{1,0:T(8,128)S(1)}, f32[64,1...) custom-call(bf16[128,8192]{1,0:T(8,128)(2,1)} %x_hbm.1, ...), custom_call_target="tpu_custom_call" | custom-call | tf_op jit(solution)/shard_map/packed/pallas_call | solution.py:951
  173.7 2.7 %finish.3 = (bf16[128,8192]{1,0:T(8,128)(2,1)}, bf16[128,8192]{1,0:T(8,128)(2,1)}, f32[64,128]{1,0:T(8,128)}, f32[64,128]{1,0:T(8,128)}, f32[64,128]{1,0:T(8,128...) custom-call(f32[8,128]{1,0:T(8,128)S(1)} %get-tuple-element.161.sums, ...), custom_call_target="tpu_custom_call" | custom-call | tf_op jit(solution)/shard_map/finish/pallas_call | solution.py:963
  177.1 0.2 conditional.1

commit v4 on v3

--- a/solution.py
+++ b/solution.py
@@ -14,7 +14,7 @@
 ROWS = 32
 AHEAD = 2
 FIRST = 4
-OUT = 4
+OUT = 6
 LEAST = 8
 
 beta_first = 0.9
@@ -324,6 +324,18 @@
         acc = lax.fori_loop(k, min(C, spread_by * k + spread_by), step, jnp.zeros((F, w), F32))
         cp[p, :, k * w : (k + 1) * w] = acc.astype(BF16)
 
+    def shrink(k):
+        with jax.named_scope("shrink"):
+            end = min(C, spread_by * k + spread_by)
+
+            def step(i, carry):
+                st[:, pl.ds(multiple(i * w, w), w)] = matches(m, k, i)
+                return carry
+
+            lax.fori_loop(k, end, step, 0)
+            part = slice(k * w, end * w)
+            igb[:, k * w : (k + 1) * w] = mm_t(ig[:, part], st[:, part]).astype(BF16)
+
     def pack_chunk(k):
         with jax.named_scope("pack_cot"):
 
@@ -398,13 +410,6 @@
 
     lax.fori_loop(0, blocks, clear, 0)
     stat[...] = jnp.zeros_like(stat)
-    if packed:
-
-        def clear_packed(i, carry):
-            igb[pl.ds(multiple(i * ROWS, ROWS), ROWS), :] = jnp.zeros((ROWS, cap), BF16)
-            return carry
-
-        lax.fori_loop(0, blocks, clear_packed, 0)
 
     ahead_of = min(FIRST, C)
     if packed:
@@ -502,9 +507,15 @@
         with jax.named_scope("wait_in"):
             wait_in(i)
 
-        @pl.when((i + AHEAD >= FIRST) & (i + AHEAD < C))
+        @pl.when((i + AHEAD >= FIRST) & (i + AHEAD < C - 1))
         def _():
             send_in(i + AHEAD)
+
+        if C > FIRST:
+
+            @pl.when(i + AHEAD == C - 2)
+            def _():
+                send_in(C - 1)
 
         for late, parts in early:
             for kind, k in parts:
@@ -559,8 +570,7 @@
             with jax.named_scope("expand"):
 
                 def grow(k, carry):
-                    st[k] = matches(m, k, i)
-                    cx[...] += mm(cb[:, pl.ds(multiple(k * w, w), w)], st[k])
+                    cx[...] += mm(cb[:, pl.ds(multiple(k * w, w), w)], matches(m, k, i))
                     return carry
 
                 cx[...] = jnp.zeros_like(cx)
@@ -641,7 +651,7 @@
                 go = grad_of(rows, j)
                 done = (gs * row_in + go).astype(BF16)
                 if packed:
-                    ig[rows, cols] = done
+                    ig[rows, lanes_of(j)] = done
                 else:
                     igb[rows, lanes_of(j)] = done
             vec[0, rows, :] = v0
@@ -650,15 +660,7 @@
         with jax.named_scope("in"):
             lax.fori_loop(0, blocks, in_rows, 0)
         if packed:
-            ig_out[:, pl.ds(multiple(m * mine + col, w), w)] = ig[pl.ds(multiple(m * F, F), F), :]
-            with jax.named_scope("shrink"):
-
-                def shrink(k, carry):
-                    cols = pl.ds(multiple(k * w, w), w)
-                    igb[:, cols] = (igb[:, cols].astype(F32) + mm_t(ig[...], st[k])).astype(BF16)
-                    return carry
-
-                lax.fori_loop(low, high_k + 1, shrink, 0)
+            ig_out[:, pl.ds(multiple(m * mine + col, w), w)] = ig[pl.ds(multiple(m * F, F), F), pl.ds(col, w)]
         return carry
 
     lax.fori_loop(0, C, work, 0)
@@ -678,10 +680,12 @@
                     while state["sent"] - state["done"] >= most:
                         wait_out(*items[state["done"]])
                         state["done"] += 1
-                    send_out(*items[state["sent"]])
+                    kind, k = items[state["sent"]]
+                    if kind and packed:
+                        shrink(k)
+                    send_out(kind, k)
                     state["sent"] += 1
 
-    pump(2)
 
     with jax.named_scope("pack"):
 
@@ -753,6 +757,7 @@
                 lax.fori_loop(0, M, round_piece, 0)
                 for copy in over_xy(o):
                     copy.start()
+    pump(2)
     with jax.named_scope("sum_xy"):
         for o in xy_order:
             for copy in over_xy(o):
@@ -778,23 +783,22 @@
             for _, _, one, two in moves:
                 one.start()
                 two.start()
-            pump(3 if bit == bits[0] else 2)
+            pump(1)
             for k, h, one, two in moves:
                 keep = flip(m, h)
                 one.wait()
                 two.wait()
                 gb[c, q, keep, 0 : 2 * dr, :] += rzg[k].astype(F32)
                 gb[c, q, keep, 2 * dr : pr, :] += rzv[k]
+            pump(1)
 
     total = gb[c, q, m]
     ga[c, q, m] = total[0 : 2 * dr, :].astype(BF16)
     with jax.named_scope("spread_z"):
-
-        def over_z(o, slot):
-            return remote(ga.at[c, q, m], ga.at[c, q, slot], az_send.at[o], az_recv.at[o], z_peer(o))
-
-        for o in z_order:
-            over_z(o, m).start()
+        first = list(spread_z(bits[-1], (ga,), az_send, az_recv))
+        for go, _ in first:
+            go.start()
+        pump(1)
         for load in loads[4:14]:
             load.wait()
         g1_out[...] = total[0:dr, :]
@@ -810,12 +814,19 @@
             m2_out[t] = two
             mem_out[t] = mem_v[t] - adam_rate * (one / corr_one) / (jnp.sqrt(two / corr_two) + adam_eps)
         sums_out[...] = total[2 * dr + tr : pr, 0:LANES if F >= LANES else F]
-        pump(len(items), len(items))
-        if packed:
-            for o in z_order[:-1]:
-                unpack_from(o)
-        for o in z_order:
-            over_z(o, flip(m, o)).wait()
+        for bit in bits[::-1]:
+            if bit != bits[-1]:
+                pump(1)
+                first = list(spread_z(bit, (ga,), az_send, az_recv))
+                for go, _ in first:
+                    go.start()
+            if bit == bits[0]:
+                pump(len(items), len(items))
+            if packed and bit == bits[0]:
+                for o in z_order[:-1]:
+                    unpack_from(o)
+            for _, come in first:
+                come.wait()
     with jax.named_scope("spread_xy"):
         for o in xy_order:
             remote(ga.at[c, q], ga.at[c, q], ax_send.at[o], ax_recv.at[o], xy_peer(o)).start()
@@ -928,7 +939,7 @@
                 return V(shape if packed else (16, LANES), dtype)
 
             scratch = [V(a.shape, a.dtype) for a in (mask, members, m1, m2, w1, w2, l1, r1, l2, r2, p1, q1, p2, q2)]
-            scratch += [only((F, R), BF16), only((M, F, cap), BF16), only((KC, w, w), BF16), only((M, F, cap), BF16)]
+            scratch += [only((F, R), BF16), only((M, F, cap), BF16), only((w, mine), BF16), only((M, F, cap), BF16)]
             scratch += [V((D, mine), BF16), V((D, cap), BF16), V((D, mine), BF16), V((D, cap), BF16)]
             scratch += [V((2, Q, M, 2 * dr, F), BF16), V((2, Q, M, tr, F), F32)]
             scratch += [V((D, D), BF16)] * 4
@@ -936,7 +947,7 @@
             scratch += [V((M * groups, LANES), F32), V((M * groups, LANES), F32)]
             scratch += [V((D, w), F32)] * 4
             scratch += [V((D, w), BF16)] * 4
-            scratch += [only((D, w), F32), only((D, w), BF16)]
+            scratch += [only((D, w), F32), only((D, mine), BF16)]
             scratch += [V((D, D), F32)] * 2
             scratch += [V((6, D, LANES), F32), V((6, K, D), F32), V((16, LANES), F32)]
             scratch += [V((2, Q, M, pr, F), F32), V((Q, M, pr, F), F32)]
@@ -947,7 +958,7 @@
             scratch += [dma((15,)), dma((2,)), dma((C,)), dma((C,)), dma((2, C)), dma((2, C)), dma((2, C)), dma((2, M))]
             scratch += [dma((2, M)), dma((2, M)), dma((2, Q)), dma((2, Q)), dma((2,)), dma((2,))]
             scratch += [dma((Q,)), dma((Q,)), dma((2, Q)), dma((2, Q)), dma((2, M)), dma((2, M))]
-            scratch += [dma((M,)), dma((M,)), dma((Q,)), dma((Q,)), dma, dma]
+            scratch += [dma((1, M)), dma((1, M)), dma((Q,)), dma((Q,)), dma, dma]
             res = pl.pallas_call(
                 functools.partial(kernel, N, M, cap),
                 out_shape=[V(a.shape, a.dtype) for a in outs],

time: 178 us -> 176 us (0.989)
  Pallas kernels: 176 us -> 174 us
where the time goes in v4:
time: 176 us
  Pallas kernels  174 us (99%)
    pallas_call x1, Pallas kernels, run(): pl.pallas_call(functools.partial(kernel, N, M, cap), out_shape=[V(a.shape...  172 us

profile of v4, /device:TPU:0, one launch (start us, length us, event | category | flops | bytes accessed | tf_op | source)
XLA Modules:
  0.0 176.1 jit_solution(18305504158175524489)
XLA Ops:
  0.6 171.7 %packed.1 = (bf16[128,8192]{1,0:T(8,128)(2,1)S(1)}, bf16[128,8192]{1,0:T(8,128)(2,1)S(1)}, f32[8,128]{1,0:T(8,128)S(1)}, f32[64,128]{1,0:T(8,128)S(1)}, f32[64,1...) custom-call(bf16[128,8192]{1,0:T(8,128)(2,1)} %x_hbm.1, ...), custom_call_target="tpu_custom_call" | custom-call | tf_op jit(solution)/shard_map/packed/pallas_call | solution.py:962
  172.3 2.7 %finish.3 = (bf16[128,8192]{1,0:T(8,128)(2,1)}, bf16[128,8192]{1,0:T(8,128)(2,1)}, f32[64,128]{1,0:T(8,128)}, f32[64,128]{1,0:T(8,128)}, f32[64,128]{1,0:T(8,128...) custom-call(f32[8,128]{1,0:T(8,128)S(1)} %get-tuple-element.161.sums, ...), custom_call_target="tpu_custom_call" | custom-call | tf_op jit(solution)/shard_map/finish/pallas_call | solution.py:974
  175.7 0.2 conditional.1

commit v5 on v4

--- a/solution.py
+++ b/solution.py
@@ -76,6 +76,7 @@
     lg_out,
     ig_out,
     sums_out,
+    order_out,
     g1_out,
     w1_out,
     l1_out,
@@ -101,7 +102,14 @@
     q1_v,
     p2_v,
     q2_v,
+    xv,
+    xp,
     cv,
+    cq,
+    order_v,
+    order_s,
+    seats_v,
+    seats_s,
     cp,
     st,
     igr,
@@ -118,6 +126,7 @@
     tab,
     stage,
     mt,
+    mp,
     mk,
     rk,
     hp,
@@ -183,7 +192,7 @@
     C = mine // w
     tiles = w // LANES
     packed = cap < mine
-    KC = cap // w
+    KC = -(-cap // w)
     groups = mine // LANES
     kb = K // N
     dr = D // N
@@ -228,60 +237,133 @@
         (q2_hbm, q2_v),
     )
     if packed:
-        pairs = (*pairs, (cot_hbm, cv))
+        pairs = (*pairs, (cot_hbm, cv), (x_hbm, xv))
     loads = [pltpu.make_async_copy(a, b, local_sem.at[i]) for i, (a, b) in enumerate(pairs)]
     for load in loads:
         load.start()
+
+    per_mask = LANES // K
+    total_tiles = M * groups
+
+    I32 = jnp.int32
+
+    def masks_to(ref):
+        loads[0].wait()
+        mt[...] = mask_v[...].T
+        ref[...] = jnp.concatenate(
+            [mt[pl.ds(j, total_tiles, stride=per_mask), :] for j in range(per_mask)], axis=1
+        )
+
+    def across(row):
+        return jnp.broadcast_to(row, (LANES, LANES)).T
+
+    def order_tiles():
+        masks_to(mp)
+        tall = jnp.concatenate([mp[...], jnp.zeros((LANES - total_tiles, LANES), I32)], axis=0)
+        count = jnp.sum(tall.T, axis=0, keepdims=True)
+        line_id = lax.broadcasted_iota(I32, (LANES, LANES), 0)
+        lane_id = lax.broadcasted_iota(I32, (LANES, LANES), 1)
+        mine_here, other = jnp.broadcast_to(count, (LANES, LANES)), across(count)
+        before = (other > mine_here) | ((other == mine_here) & (line_id < lane_id))
+        rank = jnp.sum(jnp.where(before & (line_id < total_tiles), 1, 0), axis=0, keepdims=True)
+        turn, seat = rank // M, rank % M
+        block = jnp.where(turn % 2 == 0, seat, M - 1 - seat)
+        lane = lax.broadcasted_iota(I32, (1, LANES), 1)
+        seats = jnp.where(lane < total_tiles, block * groups + turn, LANES)
+        seats_v[...] = seats
+        order_v[...] = jnp.sum(jnp.where(across(seats) == lane_id, line_id, 0), axis=0, keepdims=True)
+        order_out[...] = order_v[...]
+        to_scalars = pltpu.make_async_copy(order_v, order_s, local_sem.at[16])
+        to_scalars.start()
+        loads[15].wait()
+        to_scalars.wait()
+        deal(xv, xp, 0, 1)
+
+    def deal(src, dst, start, end, order=None):
+        order = order_s if order is None else order
+
+
+        def step(i, carry):
+            for p in range(M):
+                for j in range(tiles):
+                    t = p * groups + i * tiles + j
+                    dst[:, pl.ds(multiple(t * LANES, LANES), LANES)] = src[
+                        :, pl.ds(order[0, t] * LANES, LANES)
+                    ]
+            return carry
+
+        lax.fori_loop(start, end, step, 0)
 
     with jax.named_scope("barrier"):
         entry = pltpu.get_barrier_semaphore()
         peers = [z_peer(o) for o in z_order] + [xy_peer(o) for o in xy_order] + [core_peer]
         for peer in peers:
             pl.semaphore_signal(entry, inc=1, device_id=peer, device_id_type=MESH)
+        if packed:
+            order_tiles()
+        for load in loads[1:4]:
+            load.wait()
+        wb[c, q, m, 0:dr, :] = w1_v[...].astype(BF16)
+        wb[c, q, m, dr : 2 * dr, :] = w2_v[...].astype(BF16)
+        for t in range(6):
+            tb[c, q, m, t * kb : (t + 1) * kb, :] = mem_v[t]
         pl.semaphore_wait(entry, len(peers))
 
     kinds_in = ((xb, x_recv, 0), (cb, c_recv, 1))
+
+    def at_width(i, act):
+        if not packed:
+            act(w)
+        elif isinstance(i, int):
+            if i < KC:
+                act(min(w, cap - i * w))
+        elif cap % w == 0:
+            pl.when(i < KC)(lambda: act(w))
+        else:
+            pl.when(i < KC - 1)(lambda: act(w))
+            pl.when(i == KC - 1)(lambda: act(cap % w))
 
     def send_in(i, kinds=(0, 1)):
         here = pl.ds(multiple(m * F, F), F)
-        col = pl.ds(multiple(i * w, w), w)
-
-        def source(kind, to):
+
+        def source(kind, to, width):
             if kind and packed:
-                return cp.at[to, :, col]
-            return (x_hbm, cot_hbm)[kind].at[:, pl.ds(multiple(to * mine + i * w, w), w)]
-
-        def start(kind):
+                return cp.at[to, :, pl.ds(multiple(i * w, w), width)]
+            hbm = xp if packed else (x_hbm, cot_hbm)[kind]
+            return hbm.at[:, pl.ds(multiple(to * mine + i * w, w), width)]
+
+        def start(kind, width):
             buf, sem, _ = kinds_in[kind]
+            there = buf.at[here, pl.ds(multiple(i * w, w), width)]
             for o in z_order:
                 to = flip(m, o)
-                remote(source(kind, to), buf.at[here, col], in_send.at[kind], sem.at[i], (d, to)).start()
-            pltpu.make_async_copy(source(kind, m), buf.at[here, col], own_sem.at[kind, i]).start()
+                remote(source(kind, to, width), there, in_send.at[kind], sem.at[i], (d, to)).start()
+            pltpu.make_async_copy(source(kind, m, width), there, own_sem.at[kind, i]).start()
 
         for kind in kinds:
-            if kind and packed and not isinstance(i, int):
-                pl.when(i < KC)(lambda: start(1))
-            elif not (kind and packed) or i < KC:
-                start(kind)
+            if kind:
+                at_width(i, functools.partial(start, 1))
+            else:
+                start(0, w)
 
     others = (M - 1) * F
 
     def wait_in(i):
-        def arrive(kind):
+        def arrive(kind, width):
             buf, sem, _ = kinds_in[kind]
-            part = buf.at[pl.ds(0, others), pl.ds(0, w)]
+            part = buf.at[pl.ds(0, others), pl.ds(0, width)]
             remote(part, part, in_send.at[kind], sem.at[i], z_peer(1)).wait_recv()
-            block = buf.at[pl.ds(0, F), pl.ds(0, w)]
+            block = buf.at[pl.ds(0, F), pl.ds(0, width)]
             pltpu.make_async_copy(block, block, own_sem.at[kind, i]).wait()
 
-        arrive(0)
-        if packed:
-            pl.when(i < KC)(lambda: arrive(1))
-        else:
-            arrive(1)
+        arrive(0, w)
+        at_width(i, functools.partial(arrive, 1))
+
+    def width_of(kind, i):
+        return min(w, cap - i * w) if kind and packed else w
 
     def send_out(kind, i):
-        col = pl.ds(multiple(i * w, w), w)
+        col = pl.ds(multiple(i * w, w), width_of(kind, i))
         if kind and packed:
             there = igr.at[m, :, col]
         else:
@@ -298,7 +380,7 @@
 
     def wait_out(kind, i):
         buf = (lgb, igb)[kind]
-        part = buf.at[pl.ds(0, others), pl.ds(0, w)]
+        part = buf.at[pl.ds(0, others), pl.ds(0, width_of(kind, i))]
         remote(part, part, out_send.at[kind, i], out_recv.at[kind, 0], z_peer(1)).wait_send()
         if not (kind and packed):
             own = buf.at[pl.ds(0, F), pl.ds(0, w)]
@@ -319,7 +401,7 @@
     def pack_block(k, p):
         def step(i, acc):
             cols = pl.ds(multiple(p * mine + i * w, w), w)
-            return acc + mm_t(cv[:, cols], matches(p, k, i))
+            return acc + mm_t(cq[:, cols], matches(p, k, i))
 
         acc = lax.fori_loop(k, min(C, spread_by * k + spread_by), step, jnp.zeros((F, w), F32))
         cp[p, :, k * w : (k + 1) * w] = acc.astype(BF16)
@@ -353,23 +435,18 @@
                     return acc + mm(igr[p, :, pl.ds(multiple(k * w, w), w)], matches(p, k, i))
 
                 acc = lax.fori_loop(i // spread_by, jnp.minimum(i, KC - 1) + 1, step, jnp.zeros((F, w), F32))
-                ig_out[:, pl.ds(multiple(p * mine + i * w, w), w)] = acc.astype(BF16)
+                xv[:, pl.ds(multiple(p * mine + i * w, w), w)] = acc.astype(BF16)
                 return carry
 
             lax.fori_loop(0, C, chunk, 0)
 
     def unpack_from(o):
-        part = igr.at[0]
+        part = igr.at[0, :, pl.ds(0, cap)]
         remote(part, part, in_send.at[0], out_recv.at[1, o], z_peer(o)).wait_recv()
         unpack_block(flip(m, o))
 
-    for load in loads[:4]:
-        load.wait()
-    wb[c, q, m, 0:dr, :] = w1_v[...].astype(BF16)
-    wb[c, q, m, dr : 2 * dr, :] = w2_v[...].astype(BF16)
-    for t in range(6):
-        tb[c, q, m, t * kb : (t + 1) * kb, :] = mem_v[t]
-
+    if not packed:
+        order_out[...] = jnp.zeros_like(order_out)
     def spread_z(bit, bufs, send, recv):
         for h in range(0, M, 2 * bit):
             slot, back = flip(m, h), flip(m, h + bit)
@@ -382,12 +459,22 @@
     first = list(spread_z(bits[-1], bufs, wz_send, wz_recv))
     for go, _ in first:
         go.start()
-    per_mask = LANES // K
-    mt[...] = mask_v[...].astype(F32).T
-    mk[...] = jnp.concatenate(
-        [mt[pl.ds(j, M * groups, stride=per_mask), :] for j in range(per_mask)], axis=1
-    )
-    if packed:
+    send_in(0, (0,) if packed else (0, 1))
+    if not packed:
+        masks_to(mp)
+        mk[...] = mp[...].astype(F32)
+    else:
+        deal(xv, xp, 1, C)
+        to_seats = pltpu.make_async_copy(seats_v, seats_s, local_sem.at[17])
+        to_seats.start()
+
+        def deal_masks(t, carry):
+            for j in range(8):
+                mk[pl.ds(t * 8 + j, 1), :] = mp[pl.ds(order_s[0, t * 8 + j], 1), :].astype(F32)
+            return carry
+
+        lax.fori_loop(0, total_tiles // 8, deal_masks, 0)
+        to_seats.wait()
         flags = mk[...]
         rows, cols = M * groups, LANES
         lower = lax.broadcasted_iota(jnp.int32, (cols, cols), 0) < lax.broadcasted_iota(jnp.int32, (cols, cols), 1)
@@ -398,8 +485,6 @@
         ahead = (two < one) & (two >= one - one % groups)
         place_in = inside + mm(jnp.where(ahead, 1.0, 0.0).astype(BF16), sums)
         rk[...] = jnp.where(flags > 0.0, place_in, -1.0)
-    send_in(0, (0,) if packed else (0, 1))
-
     def clear(i, carry):
         rows = pl.ds(multiple(i * ROWS, ROWS), ROWS)
         g1[rows, :] = jnp.zeros((ROWS, D), F32)
@@ -413,7 +498,12 @@
 
     ahead_of = min(FIRST, C)
     if packed:
-        loads[-1].wait()
+        loads[14].wait()
+        deal(cv, cq, 0, C)
+        if cap % w:
+            cb[:, cap : KC * w] = jnp.zeros((D, KC * w - cap), BF16)
+            for p in range(M):
+                igr[p, :, cap : KC * w] = jnp.zeros((F, KC * w - cap), BF16)
         pack_chunk(0)
 
     def step_in(k):
@@ -660,7 +750,7 @@
         with jax.named_scope("in"):
             lax.fori_loop(0, blocks, in_rows, 0)
         if packed:
-            ig_out[:, pl.ds(multiple(m * mine + col, w), w)] = ig[pl.ds(multiple(m * F, F), F), pl.ds(col, w)]
+            xv[:, pl.ds(multiple(m * mine + col, w), w)] = ig[pl.ds(multiple(m * F, F), F), pl.ds(col, w)]
         return carry
 
     lax.fori_loop(0, C, work, 0)
@@ -833,6 +923,8 @@
         if packed:
             for o in z_order[-1:]:
                 unpack_from(o)
+            with jax.named_scope("settle"):
+                deal(xv, ig_out, 0, C, seats_s)
         for o in xy_order:
             remote(ga.at[c, q], ga.at[c, flip(q, o)], ax_send.at[o], ax_recv.at[o], xy_peer(o)).wait()
     with jax.named_scope("spread_core"):
@@ -885,21 +977,39 @@
             part = out.at[:, pl.ds(0, (M - 1) * mine)]
             remote(part, part, in_send.at[kind], out_recv.at[kind, 0], z_peer(1)).wait_recv()
         for kind, buf in enumerate((xb, cb)):
-            part = buf.at[pl.ds(0, others), :]
+            part = buf.at[pl.ds(0, others), pl.ds(0, (mine, cap)[kind])]
             remote(part, part, in_send.at[kind], out_recv.at[0, 0], z_peer(1)).wait_send()
 
 
-def finish(n_out, D, sums_ref, *refs):
+def finish(n_out, D, tiles, sums_ref, order_ref, *refs):
     outs = refs[n_out : 2 * n_out]
-    rms_ref, flag_ref, sems = refs[2 * n_out :]
+    rms_out, flag_out, order_s, rms_s, flag_s, sems = refs[2 * n_out :]
     copies = [pltpu.make_async_copy(refs[i], outs[i], sems.at[i]) for i in range(n_out)]
-    for copy in copies:
+    if tiles:
+        order = pltpu.make_async_copy(order_ref, order_s, sems.at[n_out])
+        order.start()
+    for copy in copies[1 if tiles else 0 :]:
         copy.start()
     sums = sums_ref[...]
     ratio = jnp.sqrt(sums / (sums[2:3, :] * D))
-    rms_ref[0] = ratio[0, 0]
-    rms_ref[1] = ratio[1, 0]
-    flag_ref[0] = jnp.where(sums[3, 0] > 0.0, 1, 0)
+    rms_s[0] = ratio[0, 0]
+    rms_s[1] = ratio[1, 0]
+    flag_s[0] = jnp.where(sums[3, 0] > 0.0, 1, 0)
+    for k, (src, dst) in enumerate(((rms_s, rms_out), (flag_s, flag_out))):
+        copies.append(pltpu.make_async_copy(src, dst, sems.at[n_out + 1 + k]))
+        copies[-1].start()
+    if tiles:
+        order.wait()
+
+        def step(g, carry):
+            for j in range(8):
+                t = g * 8 + j
+                here = pl.ds(multiple(t * LANES, LANES), LANES)
+                there = pl.ds(multiple(order_s[0, t] * LANES, LANES), LANES)
+                pltpu.make_async_copy(refs[0].at[:, here], outs[0].at[:, there], sems.at[0]).start()
+            return carry
+
+        lax.fori_loop(0, tiles // 8, step, 0)
     for copy in copies:
         copy.wait()
 
@@ -925,26 +1035,28 @@
         S = jax.ShapeDtypeStruct
         V = pltpu.VMEM
         dma = pltpu.SemaphoreType.DMA
-        outs = [S(x.shape, BF16), S(x.shape, BF16), S((8, min(F, LANES)), F32)]
+        outs = [S(x.shape, BF16), S(x.shape, BF16), S((8, min(F, LANES)), F32), S((1, LANES), jnp.int32)]
         outs += [S(a.shape, F32) for a in (w1, w1, l1, r1, w2, w2, l2, r2, m1, m2, members)]
         anywhere = pl.BlockSpec(memory_space=pl.ANY)
         vmem = pl.BlockSpec(memory_space=pltpu.VMEM)
-        smem = pl.BlockSpec(memory_space=pltpu.SMEM)
 
         def run(cap, number):
             packed = cap < mine
-            KC = cap // w
+            KC = -(-cap // w)
 
             def only(shape, dtype):
                 return V(shape if packed else (16, LANES), dtype)
 
             scratch = [V(a.shape, a.dtype) for a in (mask, members, m1, m2, w1, w2, l1, r1, l2, r2, p1, q1, p2, q2)]
-            scratch += [only((F, R), BF16), only((M, F, cap), BF16), only((w, mine), BF16), only((M, F, cap), BF16)]
-            scratch += [V((D, mine), BF16), V((D, cap), BF16), V((D, mine), BF16), V((D, cap), BF16)]
+            scratch += [only((F, R), BF16)] * 4
+            scratch += [V((1, LANES), jnp.int32), pltpu.SMEM((1, LANES), jnp.int32)]
+            scratch += [V((1, LANES), jnp.int32), pltpu.SMEM((1, LANES), jnp.int32)]
+            scratch += [only((M, F, KC * w), BF16), only((w, mine), BF16), only((M, F, KC * w), BF16)]
+            scratch += [V((D, mine), BF16), V((D, KC * w), BF16), V((D, mine), BF16), V((D, KC * w), BF16)]
             scratch += [V((2, Q, M, 2 * dr, F), BF16), V((2, Q, M, tr, F), F32)]
             scratch += [V((D, D), BF16)] * 4
-            scratch += [V((6, D, LANES), F32), V((6, K, D), F32), V(mask.shape[::-1], F32)]
-            scratch += [V((M * groups, LANES), F32), V((M * groups, LANES), F32)]
+            scratch += [V((6, D, LANES), F32), V((6, K, D), F32), V(mask.shape[::-1], jnp.int32)]
+            scratch += [V((M * groups, LANES), jnp.int32)] + [V((M * groups, LANES), F32)] * 2
             scratch += [V((D, w), F32)] * 4
             scratch += [V((D, w), BF16)] * 4
             scratch += [only((D, w), F32), only((D, mine), BF16)]
@@ -955,7 +1067,7 @@
             scratch += [V((M - 1, 2 * dr, F), BF16), V((M - 1, pr - 2 * dr, F), F32), V((M - 1, 2 * dr, F), BF16)]
             scratch += [V((2, Q, M, 2 * dr, F), BF16)]
             scratch += [V((D, D), BF16)] * 4
-            scratch += [dma((15,)), dma((2,)), dma((C,)), dma((C,)), dma((2, C)), dma((2, C)), dma((2, C)), dma((2, M))]
+            scratch += [dma((18,)), dma((2,)), dma((C,)), dma((C,)), dma((2, C)), dma((2, C)), dma((2, C)), dma((2, M))]
             scratch += [dma((2, M)), dma((2, M)), dma((2, Q)), dma((2, Q)), dma((2,)), dma((2,))]
             scratch += [dma((Q,)), dma((Q,)), dma((2, Q)), dma((2, Q)), dma((2, M)), dma((2, M))]
             scratch += [dma((1, M)), dma((1, M)), dma((Q,)), dma((Q,)), dma, dma]
@@ -963,26 +1075,31 @@
                 functools.partial(kernel, N, M, cap),
                 out_shape=[V(a.shape, a.dtype) for a in outs],
                 in_specs=[anywhere] * 16,
-                out_specs=[vmem] * 14,
+                out_specs=[vmem] * 15,
                 scratch_shapes=scratch,
                 compiler_params=pltpu.CompilerParams(
                     collective_id=number, has_side_effects=True, vmem_limit_bytes=46 << 20
                 ),
                 name="packed" if packed else "whole",
             )(*[pltpu.with_memory_space_constraint(a, pltpu.HBM) for a in args])
-            kept = [*res[:2], *res[3:]]
+            kept = [*res[:2], *res[4:]]
             *done, rms, flag = pl.pallas_call(
-                functools.partial(finish, len(kept), D),
+                functools.partial(finish, len(kept), D, M * groups if packed else 0),
                 out_shape=[S(a.shape, a.dtype) for a in kept] + [S((2,), F32), S((1,), jnp.int32)],
-                in_specs=[vmem] + [anywhere] * len(kept),
-                out_specs=[anywhere] * len(kept) + [smem] * 2,
-                scratch_shapes=[dma((len(kept),))],
+                in_specs=[vmem, anywhere] + [anywhere] * len(kept),
+                out_specs=[anywhere] * (len(kept) + 2),
+                scratch_shapes=[
+                    pltpu.SMEM((1, LANES), jnp.int32),
+                    pltpu.SMEM((2,), F32),
+                    pltpu.SMEM((1,), jnp.int32),
+                    dma((len(kept) + 3,)),
+                ],
                 compiler_params=pltpu.CompilerParams(vmem_limit_bytes=16 << 20),
                 name="finish",
-            )(res[2], *kept)
+            )(res[2], res[3], *kept)
             return flag, (*done, rms)
 
-        flag, fast = run(mine * 3 // 4, 0)
+        flag, fast = run(-(-mine * 11 // (16 * LANES)) * LANES, 0)
         done = lax.cond(flag[0] > 0, lambda: run(mine, 1)[1], lambda: fast)
         logits, igrad, g1, n1, l1, r1, g2, n2, l2, r2, m1, m2, new, rms = done
         return (logits, igrad, rms, g1, n1, l1, r1, g2.T, n2.T, l2.T, r2.T, m1, m2, new)

time: 176 us -> 171 us (0.972)
  Pallas kernels: 174 us -> 169 us
    pallas_call x1, Pallas kernels: 172 us -> 166 us  [run(): pl.pallas_call(functools.partial(kernel, N, M, cap), out_shape=[V(a.shape...]
where the time goes in v5:
time: 171 us; the launch traced here: 170 us
  Pallas kernels  169 us (99%)
    pallas_call x1, Pallas kernels, run(): pl.pallas_call(functools.partial(kernel, N, M, cap), out_shape=[V(a.shape...  166 us

profile of v5, /device:TPU:0, one launch (start us, length us, event | category | flops | bytes accessed | tf_op | source)
XLA Modules:
  0.0 170.3 jit_solution(11946203714234924380)
XLA Ops:
  0.6 166.4 %packed.1 = (bf16[128,8192]{1,0:T(8,128)(2,1)S(1)}, bf16[128,8192]{1,0:T(8,128)(2,1)S(1)}, f32[8,128]{1,0:T(8,128)S(1)}, s32[1,128]{1,0:T(1,128)S(1)}, f32[64,12...) custom-call(bf16[128,8192]{1,0:T(8,128)(2,1)} %x_hbm.1, ...), custom_call_target="tpu_custom_call" | custom-call | tf_op jit(solution)/shard_map/packed/pallas_call | solution.py:1074
  167.0 2.3 %finish.3 = (bf16[128,8192]{1,0:T(8,128)(2,1)}, bf16[128,8192]{1,0:T(8,128)(2,1)}, f32[64,128]{1,0:T(8,128)}, f32[64,128]{1,0:T(8,128)}, f32[64,128]{1,0:T(8,128...) custom-call(f32[8,128]{1,0:T(8,128)S(1)} %get-tuple-element.163.sums, ...), custom_call_target="tpu_custom_call" | custom-call | tf_op jit(solution)/shard_map/finish/pallas_call | solution.py:1086
  170.0 0.2 conditional.1

commit v6 on v5

--- a/solution.py
+++ b/solution.py
@@ -14,7 +14,6 @@
 ROWS = 32
 AHEAD = 2
 FIRST = 4
-OUT = 6
 LEAST = 8
 
 beta_first = 0.9
@@ -159,11 +158,8 @@
     g2ft,
     local_sem,
     in_send,
-    x_recv,
-    c_recv,
-    own_sem,
+    in_recv,
     out_send,
-    out_own,
     out_recv,
     wz_send,
     wz_recv,
@@ -265,11 +261,13 @@
         lane_id = lax.broadcasted_iota(I32, (LANES, LANES), 1)
         mine_here, other = jnp.broadcast_to(count, (LANES, LANES)), across(count)
         before = (other > mine_here) | ((other == mine_here) & (line_id < lane_id))
-        rank = jnp.sum(jnp.where(before & (line_id < total_tiles), 1, 0), axis=0, keepdims=True)
+        dealt = (line_id < total_tiles) & (line_id % groups != 0)
+        rank = jnp.sum(jnp.where(before & dealt, 1, 0), axis=0, keepdims=True)
         turn, seat = rank // M, rank % M
         block = jnp.where(turn % 2 == 0, seat, M - 1 - seat)
         lane = lax.broadcasted_iota(I32, (1, LANES), 1)
-        seats = jnp.where(lane < total_tiles, block * groups + turn, LANES)
+        seats = jnp.where(lane % groups == 0, lane, block * groups + 1 + turn)
+        seats = jnp.where(lane < total_tiles, seats, LANES)
         seats_v[...] = seats
         order_v[...] = jnp.sum(jnp.where(across(seats) == lane_id, line_id, 0), axis=0, keepdims=True)
         order_out[...] = order_v[...]
@@ -299,8 +297,6 @@
         peers = [z_peer(o) for o in z_order] + [xy_peer(o) for o in xy_order] + [core_peer]
         for peer in peers:
             pl.semaphore_signal(entry, inc=1, device_id=peer, device_id_type=MESH)
-        if packed:
-            order_tiles()
         for load in loads[1:4]:
             load.wait()
         wb[c, q, m, 0:dr, :] = w1_v[...].astype(BF16)
@@ -309,7 +305,7 @@
             tb[c, q, m, t * kb : (t + 1) * kb, :] = mem_v[t]
         pl.semaphore_wait(entry, len(peers))
 
-    kinds_in = ((xb, x_recv, 0), (cb, c_recv, 1))
+    kinds_in = (xb, cb)
 
     def at_width(i, act):
         if not packed:
@@ -323,6 +319,18 @@
             pl.when(i < KC - 1)(lambda: act(w))
             pl.when(i == KC - 1)(lambda: act(cap % w))
 
+    def send_tile(j, src):
+        here = pl.ds(multiple(m * F, F), F)
+        there = xb.at[here, j * LANES : (j + 1) * LANES]
+
+        def tile(to):
+            return src.at[:, pl.ds(multiple(to * mine + j * LANES, LANES), LANES)]
+
+        for o in z_order:
+            to = flip(m, o)
+            remote(tile(to), there, in_send.at[0], in_recv.at[0], (d, to)).start()
+        pltpu.make_async_copy(tile(m), there, in_recv.at[0]).start()
+
     def send_in(i, kinds=(0, 1)):
         here = pl.ds(multiple(m * F, F), F)
 
@@ -333,12 +341,11 @@
             return hbm.at[:, pl.ds(multiple(to * mine + i * w, w), width)]
 
         def start(kind, width):
-            buf, sem, _ = kinds_in[kind]
-            there = buf.at[here, pl.ds(multiple(i * w, w), width)]
+            there = kinds_in[kind].at[here, pl.ds(multiple(i * w, w), width)]
             for o in z_order:
                 to = flip(m, o)
-                remote(source(kind, to, width), there, in_send.at[kind], sem.at[i], (d, to)).start()
-            pltpu.make_async_copy(source(kind, m, width), there, own_sem.at[kind, i]).start()
+                remote(source(kind, to, width), there, in_send.at[kind], in_recv.at[i], (d, to)).start()
+            pltpu.make_async_copy(source(kind, m, width), there, in_recv.at[i]).start()
 
         for kind in kinds:
             if kind:
@@ -349,15 +356,13 @@
     others = (M - 1) * F
 
     def wait_in(i):
-        def arrive(kind, width):
-            buf, sem, _ = kinds_in[kind]
-            part = buf.at[pl.ds(0, others), pl.ds(0, width)]
-            remote(part, part, in_send.at[kind], sem.at[i], z_peer(1)).wait_recv()
-            block = buf.at[pl.ds(0, F), pl.ds(0, width)]
-            pltpu.make_async_copy(block, block, own_sem.at[kind, i]).wait()
-
-        arrive(0, w)
-        at_width(i, functools.partial(arrive, 1))
+        def arrive(width):
+            part = xb.at[:, pl.ds(0, w + width)]
+            remote(part, part, in_send.at[0], in_recv.at[i], z_peer(1)).wait_recv()
+
+        at_width(i, arrive)
+        if packed:
+            pl.when(i >= KC)(lambda: arrive(0))
 
     def width_of(kind, i):
         return min(w, cap - i * w) if kind and packed else w
@@ -372,19 +377,9 @@
         for o in z_order:
             to = flip(m, o)
             recv = out_recv.at[kind, o] if kind and packed else out_recv.at[kind, 0]
-            remote(
-                buf.at[pl.ds(multiple(to * F, F), F), col], there, out_send.at[kind, i], recv, (d, to)
-            ).start()
+            remote(buf.at[pl.ds(multiple(to * F, F), F), col], there, out_send.at[kind], recv, (d, to)).start()
         if not (kind and packed):
-            pltpu.make_async_copy(buf.at[pl.ds(multiple(m * F, F), F), col], there, out_own.at[kind, i]).start()
-
-    def wait_out(kind, i):
-        buf = (lgb, igb)[kind]
-        part = buf.at[pl.ds(0, others), pl.ds(0, width_of(kind, i))]
-        remote(part, part, out_send.at[kind, i], out_recv.at[kind, 0], z_peer(1)).wait_send()
-        if not (kind and packed):
-            own = buf.at[pl.ds(0, F), pl.ds(0, w)]
-            pltpu.make_async_copy(own, own, out_own.at[kind, i]).wait()
+            pltpu.make_async_copy(buf.at[pl.ds(multiple(m * F, F), F), col], there, out_recv.at[kind, 0]).start()
 
     line = lax.broadcasted_iota(jnp.int32, (w, LANES), 0).astype(F32)
 
@@ -447,19 +442,36 @@
 
     if not packed:
         order_out[...] = jnp.zeros_like(order_out)
-    def spread_z(bit, bufs, send, recv):
-        for h in range(0, M, 2 * bit):
-            slot, back = flip(m, h), flip(m, h + bit)
+    class SpreadZ:
+        def __init__(self, bit, bufs, send, recv):
+            self.go, self.come = [], []
+            offsets = list(range(0, M, 2 * bit))
             for k, buf in enumerate(bufs):
-                one, two = buf.at[c, q, slot], buf.at[c, q, back]
-                sems = (send.at[k, h + bit], recv.at[k, h + bit], z_peer(bit))
-                yield remote(one, one, *sems), remote(one, two, *sems)
+                sems = (send.at[k, bits.index(bit)], recv.at[k, bits.index(bit)], z_peer(bit))
+                for h in offsets:
+                    slot = buf.at[c, q, flip(m, h)]
+                    self.go.append(remote(slot, slot, *sems))
+                both = buf.at[c, q, pl.ds(0, len(offsets))]
+                self.come.append(remote(both, both, *sems))
+
+        def start(self):
+            for copy in self.go:
+                copy.start()
+
+        def wait(self):
+            for copy in self.come:
+                copy.wait()
 
     bufs = (wb, tb)
-    first = list(spread_z(bits[-1], bufs, wz_send, wz_recv))
-    for go, _ in first:
-        go.start()
-    send_in(0, (0,) if packed else (0, 1))
+    first = SpreadZ(bits[-1], bufs, wz_send, wz_recv)
+    first.start()
+    if packed:
+        send_tile(0, x_hbm)
+        order_tiles()
+        for j in range(1, tiles):
+            send_tile(j, xp)
+    else:
+        send_in(0)
     if not packed:
         masks_to(mp)
         mk[...] = mp[...].astype(F32)
@@ -520,22 +532,20 @@
     with jax.named_scope("weights_z"):
         for bit in bits[::-1]:
             if bit != bits[-1]:
-                first = list(spread_z(bit, bufs, wz_send, wz_recv))
-                for go, _ in first:
-                    go.start()
+                first = SpreadZ(bit, bufs, wz_send, wz_recv)
+                first.start()
             if bit == bits[0]:
                 step_in(0)
-            for _, come in first:
-                come.wait()
+            first.wait()
     with jax.named_scope("weights_xy"):
         for o in xy_order:
             for k, buf in enumerate(bufs):
-                remote(buf.at[c, q], buf.at[c, q], wx_send.at[k, o], wx_recv.at[k, o], xy_peer(o)).start()
+                remote(buf.at[c, q], buf.at[c, q], wx_send.at[k], wx_recv.at[k], xy_peer(o)).start()
         step_in(1)
         step_in(2)
-        for o in xy_order:
-            for k, buf in enumerate(bufs):
-                remote(buf.at[c, q], buf.at[c, flip(q, o)], wx_send.at[k, o], wx_recv.at[k, o], xy_peer(o)).wait()
+        for k, buf in enumerate(bufs):
+            rest = buf.at[c, pl.ds(0, Q - 1)]
+            remote(rest, rest, wx_send.at[k], wx_recv.at[k], xy_peer(1)).wait()
     with jax.named_scope("weights_core"):
         for k, buf in enumerate(bufs):
             remote(buf.at[c], buf.at[c], wc_send.at[k], wc_recv.at[k], core_peer).start()
@@ -761,21 +771,15 @@
         items += [(1, k) for k in range(KC)] + [(0, i) for i in range(3, C)]
     else:
         items += [(kind, i) for i in range(2, C) for kind in range(2)]
-    state = {"sent": already, "done": 0}
-
-    def pump(count, most=OUT):
+    state = {"sent": already}
+
+    def pump(count):
         with jax.named_scope("pump"):
-            for _ in range(count):
-                if state["sent"] < len(items):
-                    while state["sent"] - state["done"] >= most:
-                        wait_out(*items[state["done"]])
-                        state["done"] += 1
-                    kind, k = items[state["sent"]]
-                    if kind and packed:
-                        shrink(k)
-                    send_out(kind, k)
-                    state["sent"] += 1
-
+            for kind, k in items[state["sent"] : state["sent"] + count]:
+                if kind and packed:
+                    shrink(k)
+                send_out(kind, k)
+            state["sent"] += count
 
     with jax.named_scope("pack"):
 
@@ -830,7 +834,7 @@
 
         def over_xy(o):
             k = flip(q, o)
-            sems = [(gx_send.at[n, o], gx_recv.at[n, o], xy_peer(o)) for n in range(2)]
+            sems = [(gx_send.at[n], gx_recv.at[n], xy_peer(o)) for n in range(2)]
             tail = gb.at[c, k, :, pl.ds(2 * dr, pr - 2 * dr), :]
             return remote(xs.at[o], rxg.at[o], *sems[0]), remote(tail, rxv.at[o], *sems[1])
 
@@ -849,9 +853,10 @@
                     copy.start()
     pump(2)
     with jax.named_scope("sum_xy"):
+        for n, buf in enumerate((rxg, rxv)):
+            rest = buf.at[pl.ds(1, Q - 1)]
+            remote(rest, rest, gx_send.at[n], gx_recv.at[n], xy_peer(1)).wait()
         for o in xy_order:
-            for copy in over_xy(o):
-                copy.wait()
 
             def step(j, carry):
                 gb[c, q, j, 0 : 2 * dr, :] += rxg[o, j].astype(F32)
@@ -861,12 +866,13 @@
             lax.fori_loop(0, M, step, 0)
     with jax.named_scope("sum_z"):
         slot = 0
-        for bit in bits:
+        for stage, bit in enumerate(bits):
             moves = []
+            at = slot
             for h in range(0, M, 2 * bit):
                 away = flip(m, h + bit)
                 zs[slot] = gb[c, q, away, 0 : 2 * dr, :].astype(BF16)
-                sems = [(gz_send.at[k, slot], gz_recv.at[k, slot], z_peer(bit)) for k in range(2)]
+                sems = [(gz_send.at[k, stage], gz_recv.at[k, stage], z_peer(bit)) for k in range(2)]
                 tail = gb.at[c, q, away, pl.ds(2 * dr, pr - 2 * dr), :]
                 moves.append((slot, h, remote(zs.at[slot], rzg.at[slot], *sems[0]), remote(tail, rzv.at[slot], *sems[1])))
                 slot += 1
@@ -874,10 +880,11 @@
                 one.start()
                 two.start()
             pump(1)
-            for k, h, one, two in moves:
+            for k, buf in enumerate((rzg, rzv)):
+                rest = buf.at[pl.ds(at, len(moves))]
+                remote(rest, rest, gz_send.at[k, stage], gz_recv.at[k, stage], z_peer(bit)).wait()
+            for k, h, _, _ in moves:
                 keep = flip(m, h)
-                one.wait()
-                two.wait()
                 gb[c, q, keep, 0 : 2 * dr, :] += rzg[k].astype(F32)
                 gb[c, q, keep, 2 * dr : pr, :] += rzv[k]
             pump(1)
@@ -885,9 +892,8 @@
     total = gb[c, q, m]
     ga[c, q, m] = total[0 : 2 * dr, :].astype(BF16)
     with jax.named_scope("spread_z"):
-        first = list(spread_z(bits[-1], (ga,), az_send, az_recv))
-        for go, _ in first:
-            go.start()
+        first = SpreadZ(bits[-1], (ga,), az_send, az_recv)
+        first.start()
         pump(1)
         for load in loads[4:14]:
             load.wait()
@@ -907,26 +913,24 @@
         for bit in bits[::-1]:
             if bit != bits[-1]:
                 pump(1)
-                first = list(spread_z(bit, (ga,), az_send, az_recv))
-                for go, _ in first:
-                    go.start()
+                first = SpreadZ(bit, (ga,), az_send, az_recv)
+                first.start()
             if bit == bits[0]:
-                pump(len(items), len(items))
+                pump(len(items))
             if packed and bit == bits[0]:
                 for o in z_order[:-1]:
                     unpack_from(o)
-            for _, come in first:
-                come.wait()
+            first.wait()
     with jax.named_scope("spread_xy"):
         for o in xy_order:
-            remote(ga.at[c, q], ga.at[c, q], ax_send.at[o], ax_recv.at[o], xy_peer(o)).start()
+            remote(ga.at[c, q], ga.at[c, q], ax_send, ax_recv, xy_peer(o)).start()
         if packed:
             for o in z_order[-1:]:
                 unpack_from(o)
             with jax.named_scope("settle"):
                 deal(xv, ig_out, 0, C, seats_s)
-        for o in xy_order:
-            remote(ga.at[c, q], ga.at[c, flip(q, o)], ax_send.at[o], ax_recv.at[o], xy_peer(o)).wait()
+        rest = ga.at[c, pl.ds(0, Q - 1)]
+        remote(rest, rest, ax_send, ax_recv, xy_peer(1)).wait()
     with jax.named_scope("spread_core"):
         remote(ga.at[c], ga.at[c], ac_send, ac_recv, core_peer).start()
         remote(ga.at[c], ga.at[1 - c], ac_send, ac_recv, core_peer).wait()
@@ -970,12 +974,11 @@
         w2_out[...] = stepped(w2_v, q2_v, g2ft, p2_v)
 
     with jax.named_scope("drain"):
-        while state["done"] < len(items):
-            wait_out(*items[state["done"]])
-            state["done"] += 1
         for kind, out in enumerate((lg_out,) if packed else (lg_out, ig_out)):
-            part = out.at[:, pl.ds(0, (M - 1) * mine)]
-            remote(part, part, in_send.at[kind], out_recv.at[kind, 0], z_peer(1)).wait_recv()
+            remote(out, out, in_send.at[kind], out_recv.at[kind, 0], z_peer(1)).wait_recv()
+        for kind, buf in enumerate((lgb, igb)):
+            part = buf.at[pl.ds(0, others), pl.ds(0, (mine, cap)[kind])]
+            remote(part, part, out_send.at[kind], out_recv.at[0, 0], z_peer(1)).wait_send()
         for kind, buf in enumerate((xb, cb)):
             part = buf.at[pl.ds(0, others), pl.ds(0, (mine, cap)[kind])]
             remote(part, part, in_send.at[kind], out_recv.at[0, 0], z_peer(1)).wait_send()
@@ -1067,10 +1070,11 @@
             scratch += [V((M - 1, 2 * dr, F), BF16), V((M - 1, pr - 2 * dr, F), F32), V((M - 1, 2 * dr, F), BF16)]
             scratch += [V((2, Q, M, 2 * dr, F), BF16)]
             scratch += [V((D, D), BF16)] * 4
-            scratch += [dma((18,)), dma((2,)), dma((C,)), dma((C,)), dma((2, C)), dma((2, C)), dma((2, C)), dma((2, M))]
-            scratch += [dma((2, M)), dma((2, M)), dma((2, Q)), dma((2, Q)), dma((2,)), dma((2,))]
-            scratch += [dma((Q,)), dma((Q,)), dma((2, Q)), dma((2, Q)), dma((2, M)), dma((2, M))]
-            scratch += [dma((1, M)), dma((1, M)), dma((Q,)), dma((Q,)), dma, dma]
+            Z = M.bit_length() - 1
+            scratch += [dma((18,)), dma((2,)), dma((C,)), dma((2,)), dma((2, M))]
+            scratch += [dma((2, Z)), dma((2, Z)), dma((2,)), dma((2,)), dma((2,)), dma((2,))]
+            scratch += [dma((Q,)), dma((Q,)), dma((2,)), dma((2,)), dma((2, Z)), dma((2, Z))]
+            scratch += [dma((1, Z)), dma((1, Z)), dma, dma, dma, dma]
             res = pl.pallas_call(
                 functools.partial(kernel, N, M, cap),
                 out_shape=[V(a.shape, a.dtype) for a in outs],

time: 171 us -> 169 us (0.988)
  Pallas kernels: 169 us -> 167 us
where the time goes in v6:
time: 169 us
  Pallas kernels  167 us (99%)
    pallas_call x1, Pallas kernels, run(): pl.pallas_call(functools.partial(kernel, N, M, cap), out_shape=[V(a.shape...  165 us

profile of v6, /device:TPU:0, one launch (start us, length us, event | category | flops | bytes accessed | tf_op | source)
XLA Modules:
  0.0 169.1 jit_solution(5791953824093336783)
XLA Ops:
  0.6 165.1 %packed.1 = (bf16[128,8192]{1,0:T(8,128)(2,1)S(1)}, bf16[128,8192]{1,0:T(8,128)(2,1)S(1)}, f32[8,128]{1,0:T(8,128)S(1)}, s32[1,128]{1,0:T(1,128)S(1)}, f32[64,12...) custom-call(bf16[128,8192]{1,0:T(8,128)(2,1)} %x_hbm.1, ...), custom_call_target="tpu_custom_call" | custom-call | tf_op jit(solution)/shard_map/packed/pallas_call | solution.py:1078
  165.8 2.3 %finish.3 = (bf16[128,8192]{1,0:T(8,128)(2,1)}, bf16[128,8192]{1,0:T(8,128)(2,1)}, f32[64,128]{1,0:T(8,128)}, f32[64,128]{1,0:T(8,128)}, f32[64,128]{1,0:T(8,128...) custom-call(f32[8,128]{1,0:T(8,128)S(1)} %get-tuple-element.163.sums, ...), custom_call_target="tpu_custom_call" | custom-call | tf_op jit(solution)/shard_map/finish/pallas_call | solution.py:1090
  168.7 0.2 conditional.1

commit v7 on v6

--- a/solution.py
+++ b/solution.py
@@ -374,7 +374,7 @@
         else:
             there = (lg_out, ig_out)[kind].at[:, pl.ds(multiple(m * mine + i * w, w), w)]
         buf = (lgb, igb)[kind]
-        for o in z_order:
+        for o in z_order[::-1]:
             to = flip(m, o)
             recv = out_recv.at[kind, o] if kind and packed else out_recv.at[kind, 0]
             remote(buf.at[pl.ds(multiple(to * F, F), F), col], there, out_send.at[kind], recv, (d, to)).start()
@@ -894,7 +894,7 @@
     with jax.named_scope("spread_z"):
         first = SpreadZ(bits[-1], (ga,), az_send, az_recv)
         first.start()
-        pump(1)
+        pump(2)
         for load in loads[4:14]:
             load.wait()
         g1_out[...] = total[0:dr, :]

time: 169 us -> 169 us (level)
  no operation moved by 1% of the time
where the time goes in v7:
time: 169 us; the launch traced here: 168 us
  Pallas kernels  167 us (99%)
    pallas_call x1, Pallas kernels, run(): pl.pallas_call(functools.partial(kernel, N, M, cap), out_shape=[V(a.shape...  165 us

profile of v7, /device:TPU:0, one launch (start us, length us, event | category | flops | bytes accessed | tf_op | source)
XLA Modules:
  0.0 168.5 jit_solution(7770815425254220864)
XLA Ops:
  0.6 164.5 %packed.1 = (bf16[128,8192]{1,0:T(8,128)(2,1)S(1)}, bf16[128,8192]{1,0:T(8,128)(2,1)S(1)}, f32[8,128]{1,0:T(8,128)S(1)}, s32[1,128]{1,0:T(1,128)S(1)}, f32[64,12...) custom-call(bf16[128,8192]{1,0:T(8,128)(2,1)} %x_hbm.1, ...), custom_call_target="tpu_custom_call" | custom-call | tf_op jit(solution)/shard_map/packed/pallas_call | solution.py:1078
  165.2 2.3 %finish.3 = (bf16[128,8192]{1,0:T(8,128)(2,1)}, bf16[128,8192]{1,0:T(8,128)(2,1)}, f32[64,128]{1,0:T(8,128)}, f32[64,128]{1,0:T(8,128)}, f32[64,128]{1,0:T(8,128...) custom-call(f32[8,128]{1,0:T(8,128)S(1)} %get-tuple-element.163.sums, ...), custom_call_target="tpu_custom_call" | custom-call | tf_op jit(solution)/shard_map/finish/pallas_call | solution.py:1090
  168.1 0.2 conditional.1

commit v8 on v7

--- a/solution.py
+++ b/solution.py
@@ -234,7 +234,7 @@
     )
     if packed:
         pairs = (*pairs, (cot_hbm, cv), (x_hbm, xv))
-    loads = [pltpu.make_async_copy(a, b, local_sem.at[i]) for i, (a, b) in enumerate(pairs)]
+    loads = [pltpu.make_async_copy(a, b, local_sem.at[i if i < 6 else max(6, i - 7)]) for i, (a, b) in enumerate(pairs)]
     for load in loads:
         load.start()
 
@@ -271,7 +271,7 @@
         seats_v[...] = seats
         order_v[...] = jnp.sum(jnp.where(across(seats) == lane_id, line_id, 0), axis=0, keepdims=True)
         order_out[...] = order_v[...]
-        to_scalars = pltpu.make_async_copy(order_v, order_s, local_sem.at[16])
+        to_scalars = pltpu.make_async_copy(order_v, order_s, local_sem.at[9])
         to_scalars.start()
         loads[15].wait()
         to_scalars.wait()
@@ -376,10 +376,10 @@
         buf = (lgb, igb)[kind]
         for o in z_order[::-1]:
             to = flip(m, o)
-            recv = out_recv.at[kind, o] if kind and packed else out_recv.at[kind, 0]
+            recv = out_recv.at[o if kind and packed else kind]
             remote(buf.at[pl.ds(multiple(to * F, F), F), col], there, out_send.at[kind], recv, (d, to)).start()
         if not (kind and packed):
-            pltpu.make_async_copy(buf.at[pl.ds(multiple(m * F, F), F), col], there, out_recv.at[kind, 0]).start()
+            pltpu.make_async_copy(buf.at[pl.ds(multiple(m * F, F), F), col], there, out_recv.at[kind]).start()
 
     line = lax.broadcasted_iota(jnp.int32, (w, LANES), 0).astype(F32)
 
@@ -437,7 +437,7 @@
 
     def unpack_from(o):
         part = igr.at[0, :, pl.ds(0, cap)]
-        remote(part, part, in_send.at[0], out_recv.at[1, o], z_peer(o)).wait_recv()
+        remote(part, part, in_send.at[0], out_recv.at[o], z_peer(o)).wait_recv()
         unpack_block(flip(m, o))
 
     if not packed:
@@ -477,7 +477,7 @@
         mk[...] = mp[...].astype(F32)
     else:
         deal(xv, xp, 1, C)
-        to_seats = pltpu.make_async_copy(seats_v, seats_s, local_sem.at[17])
+        to_seats = pltpu.make_async_copy(seats_v, seats_s, local_sem.at[10])
         to_seats.start()
 
         def deal_masks(t, carry):
@@ -598,7 +598,7 @@
         return value.reshape(ROWS // 8, 8, LANES).sum(0)
 
     if packed:
-        early = [(C - 3, [(0, 0)]), (C - 2, [(0, 1)]), (C - 1, [(0, 2)])]
+        early = [(C - 2, [(0, 0)]), (C - 1, [(0, 1), (0, 2)])]
     else:
         early = [(C - 2, [(0, 0), (1, 0)]), (C - 1, [(0, 1), (1, 1)])]
 
@@ -823,7 +823,7 @@
     with jax.named_scope("sum_core"):
         for o in xy_order + [0]:
             k = flip(q, o)
-            remote(gb.at[1 - c, k], rcore.at[k], gc_send.at[o], gc_recv.at[o], core_peer).start()
+            remote(gb.at[1 - c, k], rcore.at[k], gc_send, gc_recv.at[o], core_peer).start()
 
         def add_core(k):
             def step(j, carry):
@@ -840,7 +840,7 @@
 
         for o in xy_order + [0]:
             k = flip(q, o)
-            remote(gb.at[1 - c, k], rcore.at[k], gc_send.at[o], gc_recv.at[o], core_peer).wait()
+            remote(gb.at[1 - c, k], rcore.at[k], gc_send, gc_recv.at[o], core_peer).wait_recv()
             add_core(k)
             if o:
 
@@ -895,8 +895,10 @@
         first = SpreadZ(bits[-1], (ga,), az_send, az_recv)
         first.start()
         pump(2)
-        for load in loads[4:14]:
+        for load in loads[4:6]:
             load.wait()
+        lines = 4 * dr * F // D + 2 * dr + 2 * F
+        pltpu.make_async_copy(g1.at[0:lines], g1.at[0:lines], local_sem.at[6]).wait()
         g1_out[...] = total[0:dr, :]
         g2_out[...] = total[dr : 2 * dr, :]
         corr_one = 1.0 - beta_first**STEP
@@ -932,6 +934,7 @@
         rest = ga.at[c, pl.ds(0, Q - 1)]
         remote(rest, rest, ax_send, ax_recv, xy_peer(1)).wait()
     with jax.named_scope("spread_core"):
+        remote(gb.at[1 - c], rcore, gc_send, gc_recv.at[0], core_peer).wait_send()
         remote(ga.at[c], ga.at[c], ac_send, ac_recv, core_peer).start()
         remote(ga.at[c], ga.at[1 - c], ac_send, ac_recv, core_peer).wait()
     with jax.named_scope("shampoo"):
@@ -975,13 +978,13 @@
 
     with jax.named_scope("drain"):
         for kind, out in enumerate((lg_out,) if packed else (lg_out, ig_out)):
-            remote(out, out, in_send.at[kind], out_recv.at[kind, 0], z_peer(1)).wait_recv()
+            remote(out, out, in_send.at[kind], out_recv.at[kind], z_peer(1)).wait_recv()
         for kind, buf in enumerate((lgb, igb)):
             part = buf.at[pl.ds(0, others), pl.ds(0, (mine, cap)[kind])]
-            remote(part, part, out_send.at[kind], out_recv.at[0, 0], z_peer(1)).wait_send()
+            remote(part, part, out_send.at[kind], out_recv.at[0], z_peer(1)).wait_send()
         for kind, buf in enumerate((xb, cb)):
             part = buf.at[pl.ds(0, others), pl.ds(0, (mine, cap)[kind])]
-            remote(part, part, in_send.at[kind], out_recv.at[0, 0], z_peer(1)).wait_send()
+            remote(part, part, in_send.at[kind], out_recv.at[0], z_peer(1)).wait_send()
 
 
 def finish(n_out, D, tiles, sums_ref, order_ref, *refs):
@@ -1071,9 +1074,9 @@
             scratch += [V((2, Q, M, 2 * dr, F), BF16)]
             scratch += [V((D, D), BF16)] * 4
             Z = M.bit_length() - 1
-            scratch += [dma((18,)), dma((2,)), dma((C,)), dma((2,)), dma((2, M))]
+            scratch += [dma((11,)), dma((2,)), dma((C,)), dma((2,)), dma((M,))]
             scratch += [dma((2, Z)), dma((2, Z)), dma((2,)), dma((2,)), dma((2,)), dma((2,))]
-            scratch += [dma((Q,)), dma((Q,)), dma((2,)), dma((2,)), dma((2, Z)), dma((2, Z))]
+            scratch += [dma, dma((Q,)), dma((2,)), dma((2,)), dma((2, Z)), dma((2, Z))]
             scratch += [dma((1, Z)), dma((1, Z)), dma, dma, dma, dma]
             res = pl.pallas_call(
                 functools.partial(kernel, N, M, cap),

time: 169 us -> 168 us (level)
  no operation moved by 1% of the time
where the time goes in v8:
time: 168 us
  Pallas kernels  166 us (99%)
    pallas_call x1, Pallas kernels, run(): pl.pallas_call(functools.partial(kernel, N, M, cap), out_shape=[V(a.shape...  164 us

profile of v8, /device:TPU:0, one launch (start us, length us, event | category | flops | bytes accessed | tf_op | source)
XLA Modules:
  0.0 168.1 jit_solution(278849611721984516)
XLA Ops:
  0.6 164.2 %packed.1 = (bf16[128,8192]{1,0:T(8,128)(2,1)S(1)}, bf16[128,8192]{1,0:T(8,128)(2,1)S(1)}, f32[8,128]{1,0:T(8,128)S(1)}, s32[1,128]{1,0:T(1,128)S(1)}, f32[64,12...) custom-call(bf16[128,8192]{1,0:T(8,128)(2,1)} %x_hbm.1, ...), custom_call_target="tpu_custom_call" | custom-call | tf_op jit(solution)/shard_map/packed/pallas_call | solution.py:1081
  164.8 2.3 %finish.3 = (bf16[128,8192]{1,0:T(8,128)(2,1)}, bf16[128,8192]{1,0:T(8,128)(2,1)}, f32[64,128]{1,0:T(8,128)}, f32[64,128]{1,0:T(8,128)}, f32[64,128]{1,0:T(8,128...) custom-call(f32[8,128]{1,0:T(8,128)S(1)} %get-tuple-element.163.sums, ...), custom_call_target="tpu_custom_call" | custom-call | tf_op jit(solution)/shard_map/finish/pallas_call | solution.py:1093
  167.8 0.2 conditional.1

commit v9 on v7

--- a/solution.py
+++ b/solution.py
@@ -912,7 +912,6 @@
         sums_out[...] = total[2 * dr + tr : pr, 0:LANES if F >= LANES else F]
         for bit in bits[::-1]:
             if bit != bits[-1]:
-                pump(1)
                 first = SpreadZ(bit, (ga,), az_send, az_recv)
                 first.start()
             if bit == bits[0]:

time: 169 us -> 168 us (level)
  no operation moved by 1% of the time
where the time goes in v9:
time: 168 us
  Pallas kernels  166 us (99%)
    pallas_call x1, Pallas kernels, run(): pl.pallas_call(functools.partial(kernel, N, M, cap), out_shape=[V(a.shape...  164 us

profile of v9, /device:TPU:0, one launch (start us, length us, event | category | flops | bytes accessed | tf_op | source)
XLA Modules:
  0.0 168.0 jit_solution(7302367944710817652)
XLA Ops:
  0.6 164.0 %packed.1 = (bf16[128,8192]{1,0:T(8,128)(2,1)S(1)}, bf16[128,8192]{1,0:T(8,128)(2,1)S(1)}, f32[8,128]{1,0:T(8,128)S(1)}, s32[1,128]{1,0:T(1,128)S(1)}, f32[64,12...) custom-call(bf16[128,8192]{1,0:T(8,128)(2,1)} %x_hbm.1, ...), custom_call_target="tpu_custom_call" | custom-call | tf_op jit(solution)/shard_map/packed/pallas_call | solution.py:1077
  164.7 2.3 %finish.3 = (bf16[128,8192]{1,0:T(8,128)(2,1)}, bf16[128,8192]{1,0:T(8,128)(2,1)}, f32[64,128]{1,0:T(8,128)}, f32[64,128]{1,0:T(8,128)}, f32[64,128]{1,0:T(8,128...) custom-call(f32[8,128]{1,0:T(8,128)S(1)} %get-tuple-element.163.sums, ...), custom_call_target="tpu_custom_call" | custom-call | tf_op jit(solution)/shard_map/finish/pallas_call | solution.py:1089
  167.6 0.2 conditional.1
